TPU v7x, 32 devices: a whole 2x2x4 slice. The times are simulated.
32 devices in a mesh: ctx: 16 (over z, y, x), fsdp: 2 (over core).
Axes of the slice: x: 2, y: 2, z: 4, core: 2. Of those that a mesh axis runs over, the one named last changes fastest.
Arguments:
- tokens: bfloat16 [2, 4096, 1024], P('fsdp', 'ctx'), may hold values from -6 to 6
- cotangent: bfloat16 [2, 4096, 1024], P('fsdp', 'ctx'), may hold values from -6 to 6
- sequence_adapter_index: int32 [2], P('fsdp'), may hold values from 0 to 1, as said below
- query_key_value_weight: bfloat16 [1024, 3072], P('fsdp'), may hold values from -0.1875 to 0.1875
- output_weight: bfloat16 [1024, 1024], P('fsdp'), may hold values from -6 to 6
- first_feed_weight: bfloat16 [1024, 4096], P('fsdp'), may hold values from -0.1875 to 0.1875
- second_feed_weight: bfloat16 [4096, 1024], P('fsdp'), may hold values from -0.09375 to 0.09375
- biases: float32 [5, 1024], replicated, may hold values from -1.25 to 1.25
- value_bias_vector: float32 [1024], replicated, may hold values from -0.0625 to 0.0625
- first_feed_bias: float32 [4096], replicated, may hold values from -1.25 to 1.25
- norm_gain_pair: float32 [2, 1024], replicated, may hold values from 0.5 to 1.5
- adapter_down_factors: bfloat16 [8, 4, 16, 1024], replicated, may hold values from -0.1875 to 0.1875
- output_down_factor: bfloat16 [8, 16, 1024], replicated, may hold values from -6 to 6
- adapter_up_factors: bfloat16 [8, 5, 16, 1024], replicated, may hold values from -0.75 to 0.75
- hidden_up_factor: bfloat16 [8, 16, 4096], replicated, may hold values from -0.75 to 0.75
- hidden_down_factor: bfloat16 [8, 16, 4096], replicated, may hold values from -0.09375 to 0.09375
Outputs:
- outcome: bfloat16 [2, 4096, 1024], P('fsdp', 'ctx')
- grad_tokens: float32 [2, 4096, 1024], P('fsdp', 'ctx')
- grad_lora_down: float32 [8, 4, 16, 1024], replicated
- grad_lora_out_down: float32 [8, 16, 1024], replicated
- grad_lora_up: float32 [8, 5, 16, 1024], replicated
- grad_hid_up: float32 [8, 16, 4096], replicated
- grad_hid_down: float32 [8, 16, 4096], replicated
Inputs may be any that keep to these rules, and one draw needn't show every extreme that they name: `sequence_adapter_index`: each of the values 0 .. min(8, 2) - 1 is used by the same number of sequences: 0 where 2 is 8 or more, else one.
All inputs are finite; a program needn't handle non-finite values.
Results may differ from a plain program's by a relative error of at most 0.023.
Values may be sent and summed in bfloat16 or wider, within the bound.
A program may use at most 256 MiB of HBM per device.

v0:
```python
import jax
import jax.numpy as jnp
from jax import lax
from jax.sharding import PartitionSpec as P

H = 16


EPSILON = 1e-05
HIGHEST = lax.Precision.HIGHEST


def exact_sum(form, left, right):
    return jnp.einsum(form, left, right, precision=HIGHEST, preferred_element_type=jnp.float32)


def plain_sum(form, left, right):
    return jnp.einsum(form, left, right, preferred_element_type=jnp.float32)


def layer_norm(value, gain, shift):
    center = value - jnp.mean(value, -1, keepdims=True)
    spread = jnp.mean(center * center, -1, keepdims=True)
    return center * lax.rsqrt(spread + EPSILON) * gain + shift


def attn_weights(query_key_value_weight, output_weight):
    return (
        lax.all_gather(query_key_value_weight, "fsdp", axis=0, tiled=True),
        lax.all_gather(output_weight, "fsdp", axis=0, tiled=True),
    )


def mlp_weights(first_feed_weight, second_feed_weight):
    return (
        lax.all_gather(first_feed_weight, "fsdp", axis=0, tiled=True),
        lax.all_gather(second_feed_weight, "fsdp", axis=0, tiled=True),
    )


def to_heads(input_array):
    return input_array.reshape(
        input_array.shape[0], input_array.shape[1], H, input_array.shape[2] // H
    )


def row_block(input_array, block_index, block_rows):
    return lax.dynamic_slice_in_dim(input_array, block_index * block_rows, block_rows, 1)


def block_grads(queries, grad_out, log_total, row_delta, keys_blk, values_blk):
    scores = plain_sum("sqhd,skhd->shqk", queries, keys_blk)
    probs = jnp.exp(scores - log_total[..., None])
    prob_low = probs.astype(jnp.bfloat16)
    grad_probs = plain_sum("sqhd,skhd->shqk", grad_out, values_blk)
    grad_scores = (probs * (grad_probs - row_delta[..., None])).astype(jnp.bfloat16)
    return (prob_low, grad_scores)


def attention_forward(queries_heads, keys_heads, values_heads):
    seq_count, row_count, head_count, head_size = queries_heads.shape
    length = keys_heads.shape[1]
    block_rows = min(512, length)
    block_count = length // block_rows

    def max_step(running, block_index):
        running_max, running_total = running
        scores = plain_sum(
            "sqhd,skhd->shqk", queries_heads, row_block(keys_heads, block_index, block_rows)
        )
        new_max = jnp.maximum(running_max, jnp.max(scores, -1))
        running_total = running_total * jnp.exp(running_max - new_max) + jnp.sum(
            jnp.exp(scores - new_max[..., None]), -1
        )
        return ((new_max, running_total), None)

    start_max = jnp.full((seq_count, head_count, row_count), -1e30, jnp.float32)
    start_total = jnp.zeros((seq_count, head_count, row_count), jnp.float32)
    (final_max, final_total), unused = lax.scan(
        max_step, (start_max, start_total), jnp.arange(block_count)
    )
    log_total = final_max + jnp.log(final_total)

    def value_step(running, block_index):
        scores = plain_sum(
            "sqhd,skhd->shqk", queries_heads, row_block(keys_heads, block_index, block_rows)
        )
        prob_low = jnp.exp(scores - log_total[..., None]).astype(jnp.bfloat16)
        return (
            running
            + plain_sum(
                "shqk,skhd->sqhd", prob_low, row_block(values_heads, block_index, block_rows)
            ),
            None,
        )

    context, unused = lax.scan(
        value_step, jnp.zeros(queries_heads.shape, jnp.float32), jnp.arange(block_count)
    )
    return (context, log_total)


def body(
    tokens,
    cotangent,
    sequence_adapter_index,
    query_key_value_weight,
    output_weight,
    first_feed_weight,
    second_feed_weight,
    biases,
    value_bias_vector,
    first_feed_bias,
    norm_gain_pair,
    adapter_down_factors,
    output_down_factor,
    adapter_up_factors,
    hidden_up_factor,
    hidden_down_factor,
):
    seq_count, row_count, model_width = tokens.shape
    adapter_number = adapter_down_factors.shape[0]
    picker = (
        sequence_adapter_index[:, None] == jnp.arange(adapter_number, dtype=jnp.int32)[None, :]
    ).astype(jnp.float32)

    def select_adapter(table):
        return jnp.einsum("sa,a...->s...", picker, table.astype(jnp.float32), precision=HIGHEST)

    def to_adapters(per_seq):
        return jnp.einsum("sa,s...->a...", picker, per_seq, precision=HIGHEST)

    selected_down = select_adapter(adapter_down_factors)
    selected_output = select_adapter(output_down_factor)
    selected_up = select_adapter(adapter_up_factors)
    hup_sel = select_adapter(hidden_up_factor)
    hdown_sel = select_adapter(hidden_down_factor)
    down_low = selected_down.astype(jnp.bfloat16)
    out_low = selected_output.astype(jnp.bfloat16)
    hdown_low = hdown_sel.astype(jnp.bfloat16)
    wqkv_full, wout_full = attn_weights(query_key_value_weight, output_weight)
    projected = plain_sum("std,de->ste", tokens, wqkv_full)
    down_att = plain_sum("std,sjrd->sjtr", tokens, down_low[:, :3])
    lifted = exact_sum("sjtr,sjrd->sjtd", down_att, selected_up[:, :3])
    queries = ((projected[..., :model_width] + biases[0] + lifted[:, 0]) * 0.125).astype(
        jnp.bfloat16
    )
    keys_own = (projected[..., model_width : 2 * model_width] + lifted[:, 1]).astype(jnp.bfloat16)
    values_own = (projected[..., 2 * model_width :] + value_bias_vector + lifted[:, 2]).astype(
        jnp.bfloat16
    )
    keys_all, values_all = (
        lax.all_gather(keys_own, "ctx", axis=1, tiled=True),
        lax.all_gather(values_own, "ctx", axis=1, tiled=True),
    )
    queries_heads = to_heads(queries)
    keys_heads = to_heads(keys_all)
    values_heads = to_heads(values_all)
    context, log_total = attention_forward(queries_heads, keys_heads, values_heads)
    context = context.reshape(seq_count, row_count, model_width)
    context_low = context.astype(jnp.bfloat16)
    down_out = plain_sum("std,srd->str", context_low, out_low)
    branch = (
        plain_sum("std,de->ste", context_low, wout_full)
        + biases[1]
        + exact_sum("str,srd->std", down_out, selected_up[:, 3])
    )

    def first_norm(value):
        return layer_norm(value, norm_gain_pair[0], biases[3])

    def second_norm(value):
        return layer_norm(value, norm_gain_pair[1], biases[4])

    def gelu_exact(value):
        return jax.nn.gelu(value, approximate=False)

    normed, norm_back = jax.vjp(first_norm, tokens.astype(jnp.float32) + branch)
    normed_low = normed.astype(jnp.bfloat16)
    wfc1_full, wfc2_full = mlp_weights(first_feed_weight, second_feed_weight)
    down_fc1 = plain_sum("std,srd->str", normed_low, down_low[:, 3])
    hidden_pre = (
        plain_sum("std,df->stf", normed_low, wfc1_full)
        + first_feed_bias
        + exact_sum("str,srf->stf", down_fc1, hup_sel)
    )
    activated, gelu_back = jax.vjp(gelu_exact, hidden_pre)
    act_low = activated.astype(jnp.bfloat16)
    down_fc2 = plain_sum("stf,srf->str", act_low, hdown_low)
    mixed_out = (
        plain_sum("stf,fd->std", act_low, wfc2_full)
        + biases[2]
        + exact_sum("str,srd->std", down_fc2, selected_up[:, 4])
    )
    outcome, out_back = jax.vjp(second_norm, normed + mixed_out)
    (grad_sum2,) = out_back(cotangent.astype(jnp.float32))
    grad_mixed = grad_sum2.astype(jnp.bfloat16)
    grad_up_fc2 = exact_sum("str,std->srd", down_fc2, grad_mixed)
    grad_rank_fc2 = exact_sum("std,srd->str", grad_mixed, selected_up[:, 4]).astype(jnp.bfloat16)
    grad_hdown = plain_sum("str,stf->srf", grad_rank_fc2, act_low)
    wfc1_full, wfc2_full = mlp_weights(first_feed_weight, second_feed_weight)
    grad_act = (
        plain_sum("std,fd->stf", grad_mixed, wfc2_full)
        + plain_sum("str,srf->stf", grad_rank_fc2, hdown_low)
    ).astype(jnp.bfloat16)
    (grad_hidden,) = gelu_back(grad_act.astype(jnp.float32))
    grad_hidden = grad_hidden.astype(jnp.bfloat16)
    grad_hup = exact_sum("str,stf->srf", down_fc1, grad_hidden)
    grad_rank_fc1 = exact_sum("stf,srf->str", grad_hidden, hup_sel).astype(jnp.bfloat16)
    grad_down_fc1 = plain_sum("str,std->srd", grad_rank_fc1, normed_low)
    grad_normed_low = (
        plain_sum("stf,df->std", grad_hidden, wfc1_full)
        + plain_sum("str,srd->std", grad_rank_fc1, down_low[:, 3])
    ).astype(jnp.bfloat16)
    (grad_resid,) = norm_back(grad_sum2 + grad_normed_low.astype(jnp.float32))
    mlp_hup = to_adapters(grad_hup)
    mlp_hdown = to_adapters(grad_hdown)
    mlp_fc1 = to_adapters(grad_down_fc1)
    mlp_fc2 = to_adapters(grad_up_fc2)
    mlp_hup, mlp_hdown, mlp_fc1, mlp_fc2 = lax.psum(
        (mlp_hup, mlp_hdown, mlp_fc1, mlp_fc2), ("ctx", "fsdp")
    )
    grad_branch = grad_resid.astype(jnp.bfloat16)
    grad_up_out = exact_sum("str,std->srd", down_out, grad_branch)
    grad_rank_out = exact_sum("std,srd->str", grad_branch, selected_up[:, 3]).astype(jnp.bfloat16)
    grad_out_down = plain_sum("str,std->srd", grad_rank_out, context_low)
    wqkv_full, wout_full = attn_weights(query_key_value_weight, output_weight)
    grad_context = (
        plain_sum("std,ed->ste", grad_branch, wout_full)
        + plain_sum("str,srd->std", grad_rank_out, out_low)
    ).astype(jnp.bfloat16)
    row_delta = jnp.sum(to_heads(grad_context.astype(jnp.float32) * context), -1)
    delta_heads = jnp.swapaxes(row_delta, 1, 2)
    grad_heads = to_heads(grad_context)
    length = keys_all.shape[1]
    block_rows = min(512, length)
    block_count = length // block_rows

    def key_step(block_index, running):
        grad_query, grad_key, grad_value = running
        keys_blk = row_block(keys_heads, block_index, block_rows)
        values_blk = row_block(values_heads, block_index, block_rows)
        prob_low, grad_scores = block_grads(
            queries_heads, grad_heads, log_total, delta_heads, keys_blk, values_blk
        )
        grad_query = grad_query + plain_sum("shqk,skhd->sqhd", grad_scores, keys_blk)
        grad_key = lax.dynamic_update_slice_in_dim(
            grad_key,
            plain_sum("shqk,sqhd->skhd", grad_scores, queries_heads),
            block_index * block_rows,
            1,
        )
        grad_value = lax.dynamic_update_slice_in_dim(
            grad_value,
            plain_sum("shqk,sqhd->skhd", prob_low, grad_heads),
            block_index * block_rows,
            1,
        )
        return (grad_query, grad_key, grad_value)

    start_query = jnp.zeros(queries_heads.shape, jnp.float32)
    start_keys = jnp.zeros(keys_heads.shape, jnp.float32)
    grad_query, grad_key_all, grad_value_all = lax.fori_loop(
        0, block_count, key_step, (start_query, start_keys, start_keys)
    )
    grad_keys, grad_values = (
        lax.psum_scatter(
            grad_key_all.reshape(seq_count, length, model_width).astype(jnp.bfloat16),
            "ctx",
            scatter_dimension=1,
            tiled=True,
        ).astype(jnp.float32),
        lax.psum_scatter(
            grad_value_all.reshape(seq_count, length, model_width).astype(jnp.bfloat16),
            "ctx",
            scatter_dimension=1,
            tiled=True,
        ).astype(jnp.float32),
    )
    grad_qlin = grad_query.reshape(seq_count, row_count, model_width).astype(jnp.bfloat16) * 0.125
    grad_key_low = grad_keys.astype(jnp.bfloat16)
    grad_value_low = grad_values.astype(jnp.bfloat16)
    stacked = jnp.stack([grad_qlin, grad_key_low, grad_value_low], 1)
    grad_up_att = exact_sum("sjtr,sjtd->sjrd", down_att, stacked)
    grad_rank_att = exact_sum("sjtd,sjrd->sjtr", stacked, selected_up[:, :3]).astype(jnp.bfloat16)
    grad_down_att = plain_sum("sjtr,std->sjrd", grad_rank_att, tokens)
    joined = jnp.concatenate([grad_qlin, grad_key_low, grad_value_low], -1)
    grad_tokens = (
        grad_resid
        + plain_sum("ste,de->std", joined, wqkv_full)
        + plain_sum("sjtr,sjrd->std", grad_rank_att, down_low[:, :3])
    )
    attn_down = to_adapters(grad_down_att)
    attn_out = to_adapters(grad_out_down)
    attn_up = to_adapters(jnp.concatenate([grad_up_att, grad_up_out[:, None]], 1))
    attn_down, attn_out, attn_up = lax.psum((attn_down, attn_out, attn_up), ("ctx", "fsdp"))
    total_down = jnp.concatenate([attn_down, mlp_fc1[:, None]], 1)
    total_up = jnp.concatenate([attn_up, mlp_fc2[:, None]], 1)
    return (
        outcome.astype(jnp.bfloat16),
        grad_tokens,
        total_down,
        attn_out,
        total_up,
        mlp_hup,
        mlp_hdown,
    )


def solution(mesh):
    return jax.shard_map(
        body,
        mesh=mesh,
        in_specs=(
            P("fsdp", "ctx", None),
            P("fsdp", "ctx", None),
            P("fsdp"),
            P("fsdp", None),
            P("fsdp", None),
            P("fsdp", None),
            P("fsdp", None),
            P(),
            P(),
            P(),
            P(),
            P(),
            P(),
            P(),
            P(),
            P(),
        ),
        out_specs=(P("fsdp", "ctx", None), P("fsdp", "ctx", None), P(), P(), P(), P(), P()),
        check_vma=False,
    )
```

profile of v0, /device:TPU:0, one launch (start us, length us, event | category | flops | bytes accessed | tf_op | source)
XLA Modules:
  0.0 1084.0 jit_solution(2669446677356198744)
XLA Ops:
  11.9 4.3 convolution_bitcast_fusion.2
  16.8 12.3 %all-gather.7.cloned.1.call-done = bf16[1024,3072]{1,0:T(8,128)(2,1)} async-done(((bf16[512,3072]{1,0:T(8,128)(2,1)}), bf16[1024,3072]{1,0:T(8,128)(2,1)}) %all-gather.7.cloned.1.call-update) | async-done | bytes 6291472 | tf_op jit(solution)/shard_map/all_gather | solution.py:29
  29.1 4.7 convolution_bitcast_fusion.1
  39.9 3.2 fusion.87
  43.1 3.2 fusion.85
  49.5 100.2 %all-gather.11.cloned.1.call-done = bf16[1,4096,1024]{2,1,0:T(8,128)(2,1)} async-done(((bf16[1,256,1024]{2,1,0:T(8,128)(2,1)}), bf16[1,4096,1024]{2,1,0:T(8,128)(2,1)}) %all-gather.11.cloned.1.call-update) | async-done | bytes 8388624 | tf_op jit(solution)/shard_map/all_gather | solution.py:153
  149.6 11.8 %copy.37 = bf16[1,4096,1024]{1,2,0:T(8,128)(2,1)} copy(bf16[1,4096,1024]{2,1,0:T(8,128)(2,1)} %all-gather.11.cloned.1.call-done) | data formatting | bytes 16777216 | tf_op jit(solution)/shard_map/all_gather | solution.py:153
  161.4 39.8 %while.42 = (s32[]{:T(128)}, f32[1,16,256]{2,1,0:T(8,128)S(1)}, f32[1,16,256]{2,1,0:T(8,128)S(1)}, s32[8]{0:T(128)S(1)}, bf16[1,4096,16,64]{1,3,2,0:T(8,128)(2,1...) while((s32[]{:T(128)}, f32[1,16,256]{2,1,0:T(8,128)S(1)}, ...), condition=%wide.region_3.4_spmd.clone, body=%wide.region_0.3_spmd.clone.sunk | while | flops 274747392 | bytes 18563252 | solution.py:79
  172.6 2.5 bitcast_reduce_fusion.3
  177.6 2.5 bitcast_reduce_fusion.3
  192.5 2.5 bitcast_reduce_fusion.3
  201.2 62.8 %all-gather.9.cloned.1.call-done = bf16[1,4096,1024]{2,1,0:T(8,128)(2,1)} async-done(((bf16[1,256,1024]{2,1,0:T(8,128)(2,1)}), bf16[1,4096,1024]{2,1,0:T(8,128)(2,1)}) %all-gather.9.cloned.1.call-update) | async-done | bytes 8388624 | tf_op jit(solution)/shard_map/all_gather | solution.py:154
  264.0 12.1 %copy.36 = bf16[1,4096,1024]{1,2,0:T(8,128)(2,1)} copy(bf16[1,4096,1024]{2,1,0:T(8,128)(2,1)} %all-gather.9.cloned.1.call-done) | data formatting | bytes 16777216 | tf_op jit(solution)/shard_map/all_gather | solution.py:154
  276.1 46.5 %while.43 = (s32[]{:T(128)}, f32[1,256,16,64]{1,3,2,0:T(8,128)S(1)}, s32[8]{0:T(128)S(1)}, bf16[1,4096,16,64]{1,3,2,0:T(8,128)(2,1)}, bf16[1,4096,16,64]{1,3,2,0...) while((s32[]{:T(128)}, ...), condition=%wide.region_5.6_spmd.clone, body=%wide.region_4.5_spmd.clone.sunk | while | flops 541589504 | bytes 5260984 | solution.py:97
  277.4 4.3 fusion.208
  283.0 4.8 fusion.208
  289.1 4.6 fusion.208
  294.9 4.3 fusion.208
  300.5 4.3 fusion.208
  306.1 4.8 fusion.208
  312.2 4.8 fusion.208
  318.3 4.3 fusion.208
  330.5 5.8 convolution_add_fusion.2
  336.3 14.5 %multiply_convert_fusion.1 = (bf16[256,4096]{1,0:T(8,128)(2,1)S(1)}, f32[256,4096]{1,0:T(8,128)}, f32[256,4096]{1,0:T(8,128)}) fusion(f32[256,4096]{1,0:T(8,128)S(1)} %convolution_add_fusion.2, f32[256,16]{0,1:T(8,128)S(1)} %fusion.109, f32[1,16,4096]{2,0,1:T(1,128)S(1)} %copy-done.21), kind=kOutput, calls=%fused_computation.62 | convolution fusion | flops 270532608 | bytes 14958592 | tf_op jit(solution)/shard_map/str,srf->stf/dot_general | solution.py:14
  352.8 6.5 convolution_add_fusion.8
  363.1 4.4 fusion.136
  367.6 6.0 fusion.50
  384.3 4.3 broadcast_in_dim.56.clone
  388.6 4.3 broadcast_in_dim.56
  392.9 101.9 %while.44 = (s32[]{:T(128)}, f32[1,256,16,64]{1,3,2,0:T(8,128)S(1)}, bf16[1,4096,16,64]{1,3,2,0:T(8,128)(2,1)}, bf16[1,4096,16,64]{1,3,2,0:T(8,128)(2,1)}, bf16[...) while((s32[]{:T(128)}, ...), condition=%wide.region_16.17_spmd.clone, body=%wide.region_15.16_spmd.clone.sunk | while | flops 1355284480 | bytes 49332440 | solution.py:263
  395.7 3.2 multiply_convert_fusion.3
  408.3 3.2 multiply_convert_fusion.3
  421.0 3.2 multiply_convert_fusion.3
  433.7 3.2 multiply_convert_fusion.3
  446.4 3.2 multiply_convert_fusion.3
  459.2 3.2 multiply_convert_fusion.3
  462.4 2.6 bitcast_dynamic-update-slice_fusion.5
  472.0 3.2 multiply_convert_fusion.3
  484.7 3.2 multiply_convert_fusion.3
  494.9 12.0 %copy.45 = bf16[1,4096,1024]{2,1,0:T(8,128)(2,1)} copy(bf16[1,4096,1024]{1,2,0:T(8,128)(2,1)} %bitcast.371) | data formatting | bytes 16777216 | tf_op jit(solution)/shard_map/convert_element_type | solution.py:274
  506.9 12.0 %copy.44 = bf16[1,4096,1024]{2,1,0:T(8,128)(2,1)} copy(bf16[1,4096,1024]{1,2,0:T(8,128)(2,1)} %bitcast.372) | data formatting | bytes 16777216 | tf_op jit(solution)/shard_map/convert_element_type | solution.py:268
  532.8 2.5 broadcast_multiply_fusion
  535.3 147.8 %reduce-scatter.5.cloned.1.call-done = bf16[1,256,1024]{2,1,0:T(8,128)(2,1)} async-done(((bf16[1,4096,1024]{2,1,0:T(8,128)(2,1)}), bf16[1,256,1024]{2,1,0:T(8,128)(2,1)}) %reduce-scatter.5.cloned.1.call-update) | async-done | bytes 524304 | tf_op jit(solution)/shard_map/reduce_scatter | solution.py:273
  683.1 182.6 %reduce-scatter.3.cloned.1.call-done = bf16[1,256,1024]{2,1,0:T(8,128)(2,1)} async-done(((bf16[1,4096,1024]{2,1,0:T(8,128)(2,1)}), bf16[1,256,1024]{2,1,0:T(8,128)(2,1)}) %reduce-scatter.3.cloned.1.call-update) | async-done | bytes 524304 | tf_op jit(solution)/shard_map/reduce_scatter | solution.py:267
  865.7 2.6 convolution_convert_fusion
  873.7 5.0 fusion.71
  880.0 188.5 %all-reduce.3.cloned.1.call-done = (f32[8,1,16,1024]{3,2,0,1:T(8,128)}, f32[8,3,16,1024]{3,2,1,0:T(8,128)}, f32[8,16,1024]{2,1,0:T(8,128)}, f32[8,1,16,1024]{3,2...) async-done(((f32[8,1,16,1024]{3,2,0,1:T(8,128)}, f32[8,3,16,1024]{3,2,1,0:T(8,128)}, f32[8,16,1024]{2,1,0:T(8,128)}, ...) | async-done | bytes 9437200 | tf_op jit(solution)/shard_map/psum | solution.py:220
  1068.5 3.3 pad_maximum_fusion.1
  (298 shorter events, 168.2 us)
Async XLA Ops:
  7.2 4.4 copy-start.9
  7.2 21.9 %all-gather.7.cloned.1.call-start = ((), (), s32[]{:S(2)}) async-start(), calls=%async_computation.2 | async-start | bytes 9437184 | tf_op jit(solution)/shard_map/all_gather | solution.py:29
  7.9 8.2 copy-start.44
  7.9 141.7 %all-gather.11.cloned.1.call-start = ((), (), s32[]{:S(2)}) async-start(), calls=%async_computation.4 | async-start | bytes 8912896 | tf_op jit(solution)/shard_map/all_gather | solution.py:153
  11.6 22.2 %copy-start.23 = (f32[1,3,16,1024]{3,0,2,1:T(1,128)}, f32[1,3,16,1024]{3,0,2,1:T(1,128)S(1)}, u32[]{:S(2)}) copy-start(f32[1,3,16,1024]{3,0,2,1:T(1,128)S(1)} %slice.79) | copy-start | bytes 589828
  11.9 21.9 %copy-start.29 = (f32[3,16,256]{2,1,0:T(8,128)}, f32[3,16,256]{2,1,0:T(8,128)S(1)}, u32[]{:S(2)}) copy-start(f32[3,16,256]{2,1,0:T(8,128)S(1)} %fusion.97) | copy-start | bytes 147460
  16.8 313.1 %copy-start.39 = (f32[1,1024]{1,0:T(1,128)}, f32[1,1024]{1,0:T(1,128)S(1)}, u32[]{:S(2)}) copy-start(f32[1,1024]{1,0:T(1,128)S(1)} %get-tuple-element.432) | copy-start | bytes 12292
  16.8 17.0 %copy-start.48 = (f32[1024]{0:T(1024)S(1)}, f32[1024]{0:T(1024)}, u32[]{:S(2)}) copy-start(f32[1024]{0:T(1024)} %param.30) | copy-start | bytes 12292
  29.1 4.8 copy-start.2
  35.5 228.6 %all-gather.9.cloned.1.call-start = ((), (), s32[]{:S(2)}) async-start(), calls=%async_computation.3 | async-start | bytes 8912896 | tf_op jit(solution)/shard_map/all_gather | solution.py:154
  36.2 289.8 %all-gather.13.cloned.1.call-start = ((), (), s32[]{:S(2)}) async-start(), calls=%async_computation.5 | async-start | bytes 3145728 | tf_op jit(solution)/shard_map/all_gather | solution.py:30
  36.8 293.6 %all-gather.15.cloned.1.call-start = ((), (), s32[]{:S(2)}) async-start(), calls=%async_computation.6 | async-start | bytes 12582912 | tf_op jit(solution)/shard_map/all_gather | solution.py:36
  37.4 315.3 %all-gather.17.cloned.1.call-start = ((), (), s32[]{:S(2)}) async-start(), calls=%async_computation.7 | async-start | bytes 12582912 | tf_op jit(solution)/shard_map/all_gather | solution.py:37
  38.0 645.1 %reduce-scatter.5.cloned.1.call-start = ((), (), s32[]{:S(2)}) async-start(), calls=%async_computation.9 | async-start | bytes 8912896 | tf_op jit(solution)/shard_map/reduce_scatter | solution.py:273
  38.7 291.2 %copy-start.36 = (f32[1,1024]{1,0:T(1,128)}, f32[1,1024]{1,0:T(1,128)S(1)}, u32[]{:S(2)}) copy-start(f32[1,1024]{1,0:T(1,128)S(1)} %get-tuple-element.437) | copy-start | bytes 12292
  326.1 4.1 copy-start.31
  330.2 6.1 copy-start.12
  330.4 5.8 copy-start.38
  330.4 5.8 copy-start.21
  336.3 15.8 %copy-start.25 = (bf16[1,16,4096]{2,0,1:T(2,128)(2,1)S(1)}, bf16[1,16,4096]{2,0,1:T(2,128)(2,1)}, u32[]{:S(2)}) copy-start(bf16[1,16,4096]{2,0,1:T(2,128)(2,1)} %fusion.85) | copy-start | bytes 393220
  336.3 16.5 %copy-start.49 = (f32[1,1024]{1,0:T(1,128)S(1)}, f32[1,1024]{1,0:T(1,128)}, u32[]{:S(2)}) copy-start(f32[1,1024]{1,0:T(1,128)} %get-tuple-element.435) | copy-start | bytes 12292
  352.7 10.3 slice-start.2
  352.8 6.6 copy-start.37
  352.8 6.6 copy-start.40
  352.8 7.9 copy-start.20
  352.8 7.9 copy-start.41
  352.8 10.3 slice-start.3
  362.4 13.0 %slice-start = ((s8[8388608]{0:T(1024)(128)(4,1)}), s8[4194304]{0:T(1024)(128)(4,1)S(1)}, s32[]{:S(2)}) async-start(s8[8388608]{0:T(1024)(128)(4,1)} %bitcast.399), calls=%async_computation.11 | async-start | bytes 8388608
  362.5 5.0 copy-start.13
  363.1 4.5 copy-start.42
  363.1 4.5 copy-start.26
  363.1 12.3 %slice-start.1 = ((s8[8388608]{0:T(1024)(128)(4,1)}), s8[4194304]{0:T(1024)(128)(4,1)S(1)}, s32[]{:S(2)}) async-start(s8[8388608]{0:T(1024)(128)(4,1)} %bitcast.399), calls=%async_computation.12 | async-start | bytes 8388608
  367.5 6.1 copy-start.22
  373.6 4.2 copy-start.4
  506.9 358.8 %reduce-scatter.3.cloned.1.call-start = ((), (), s32[]{:S(2)}) async-start(), calls=%async_computation.8 | async-start | bytes 8912896 | tf_op jit(solution)/shard_map/reduce_scatter | solution.py:267
  519.0 549.5 %all-reduce.3.cloned.1.call-start = ((), (), s32[]{:S(2)}) async-start(), calls=%async_computation.10 | async-start | bytes 18874368 | tf_op jit(solution)/shard_map/psum | solution.py:220
  520.5 10.7 copy-start.5
  522.6 7.4 copy-start.7
  524.1 8.6 copy-start.46
  530.0 335.7 %copy-start.24 = (f32[1,3,16,1024]{3,0,2,1:T(1,128)S(1)}, f32[1,3,16,1024]{3,0,2,1:T(1,128)}, u32[]{:S(2)}) copy-start(f32[1,3,16,1024]{3,0,2,1:T(1,128)} %copy-done.23) | copy-start | bytes 589828
  532.8 335.5 %copy-start.30 = (f32[3,16,256]{2,1,0:T(8,128)S(1)}, f32[3,16,256]{2,1,0:T(8,128)}, u32[]{:S(2)}) copy-start(f32[3,16,256]{2,1,0:T(8,128)} %copy-done.29) | copy-start | bytes 147460
  535.3 333.7 %copy-start.10 = (bf16[1,256,1024]{2,1,0:T(8,128)(2,1)S(1)}, bf16[1,256,1024]{2,1,0:T(8,128)(2,1)}, u32[]{:S(2)}) copy-start(bf16[1,256,1024]{2,1,0:T(8,128)(2,1)} %param.22) | copy-start | bytes 1572868
  683.1 185.2 %copy-start.53 = (bf16[1,256,1024]{2,1,0:T(8,128)(2,1)S(1)}, bf16[1,256,1024]{2,1,0:T(8,128)(2,1)}, u32[]{:S(2)}) copy-start(bf16[1,256,1024]{2,1,0:T(8,128)(2,1)} %reduce-scatter.5.cloned.1.call-done) | copy-start | bytes 1572868
  865.7 3.6 copy-start.47
  868.3 4.1 copy-start.32
  873.7 5.0 copy-start.33
  1068.5 5.0 copy-start.28
  1071.8 3.8 copy-start.17
  (20 other events, 40.9 us)
Sparse Core Ops, SparseCore 0:
  9.6 19.4 all-gather.6
  35.6 113.9 all-gather.10
  153.0 111.0 all-gather.8
  265.4 8.7 all-gather.12
  275.6 21.0 all-gather.14
  298.1 21.0 all-gather.16
  507.0 176.0 reduce-scatter.4
  685.4 180.2 reduce-scatter.2
  872.7 195.7 all-reduce.2
where the time goes:
time: 1090 us; the launch traced here: 1080 us
  waiting for transfers between devices  697 us (64%)
  matrix products  247 us (23%)
  local copies, waits for them, and re-layouts  81.7 us (7%)
  other arithmetic  30.3 us (3%)
  between operations  15.8 us (1%)
  loops' own time  11.6 us (1%)
    dot_general x76, matrix products, plain_sum(): return jnp.einsum(form, left, right, preferred_element_type=jnp.float32)  204 us
    psum x1, waiting for transfers between devices, body(): lax.psum((mlp_hup, mlp_hdown, mlp_fc1, mlp_fc2), ('ctx', 'fsdp'))  189 us
    reduce_scatter x1, waiting for transfers between devices, body(): lax.psum_scatter(grad_key_all.reshape(seq_count, length, model_width).ast...  183 us
    reduce_scatter x1, waiting for transfers between devices, body(): lax.psum_scatter(grad_value_all.reshape(seq_count, length, model_width).a...  148 us
    all_gather x1, waiting for transfers between devices, body(): lax.all_gather(keys_own, 'ctx', axis=1, tiled=True)  100 us
    all_gather x1, waiting for transfers between devices, body(): lax.all_gather(values_own, 'ctx', axis=1, tiled=True)  62.8 us
    dot_general x12, matrix products, exact_sum(): jnp.einsum(form, left, right, precision=HIGHEST, preferred_element_type=j...  31.9 us
  transfers between devices with their start and end apart: 9, of which 6 were waited for; matrix products, arithmetic and copies ran while one was open for 17% of the time, Pallas kernels for 0%

commit v1 on v0

--- a/solution.py
+++ b/solution.py
@@ -1,6 +1,10 @@
+import functools
+
 import jax
 import jax.numpy as jnp
 from jax import lax
+from jax.experimental import pallas as pl
+from jax.experimental.pallas import tpu as pltpu
 from jax.sharding import PartitionSpec as P
 
 H = 16
@@ -100,7 +104,7 @@
     return (context, log_total)
 
 
-def body(
+def gather_body(
     tokens,
     cotangent,
     sequence_adapter_index,
@@ -307,9 +311,357 @@
     )
 
 
+BF16 = jnp.bfloat16
+F32 = jnp.float32
+LOG2E = 1.4426950408889634
+VMEM_LIMIT = 56 * 2**20
+
+
+def dot32(left, right):
+    return jnp.dot(left, right, preferred_element_type=F32)
+
+
+def split_three(value):
+    high = value.astype(BF16)
+    rest = value - high.astype(F32)
+    middle = rest.astype(BF16)
+    return high, middle, (rest - middle.astype(F32)).astype(BF16)
+
+
+def flip(value):
+    return value.astype(F32).T.astype(BF16)
+
+
+def forward_kernel(block_q, block_k, qkv_ref, send_ref, context_ref, lse_ref, qta, kk, vta, scores):
+    peers, _, rows = qkv_ref.shape
+    length = peers * rows
+
+    def prepare(j, _):
+        cols = pl.ds(pl.multiple_of(j * rows, rows), rows)
+        query = qkv_ref[j, 0:64, :].astype(F32) * LOG2E
+        high = query.astype(BF16)
+        qta[0:64, cols] = high
+        qta[64:128, cols] = (query - high.astype(F32)).astype(BF16)
+        key = qkv_ref[j, 64:128, :]
+        kk[cols, :] = flip(jnp.concatenate([key, key], 0))
+        vta[0:64, cols] = qkv_ref[j, 128:192, :]
+        vta[64:80, cols] = (lax.broadcasted_iota(jnp.int32, (16, rows), 0) == 0).astype(F32).astype(BF16)
+        return 0
+
+    lax.fori_loop(0, peers, prepare, 0)
+    steps = length // block_k
+
+    def query_step(i, _):
+        cols = pl.ds(pl.multiple_of(i * block_q, block_q), block_q)
+        query = qta[:, cols]
+        scores[0] = dot32(kk[pl.ds(0, block_k), :], query)
+
+        def half(j, now, carry):
+            running, total = carry
+            later = jnp.minimum(j + 1, steps - 1)
+            here = pl.ds(pl.multiple_of(j * block_k, block_k), block_k)
+            there = pl.ds(pl.multiple_of(later * block_k, block_k), block_k)
+            scores[1 - now] = dot32(kk[there, :], query)
+            block = scores[now]
+            new = jnp.maximum(running, jnp.max(block, 0, keepdims=True))
+            weights = jnp.exp2(block - new).astype(BF16)
+            return new, total * jnp.exp2(running - new) + dot32(vta[:, here], weights)
+
+        def pair(j, carry):
+            return half(2 * j + 1, 1, half(2 * j, 0, carry))
+
+        start = (jnp.full((1, block_q), -jnp.inf, F32), jnp.zeros((80, block_q), F32))
+        top, total = lax.fori_loop(0, steps // 2, pair, start)
+        weight_sum = total[64:65]
+        context = total[0:64] / weight_sum
+        context_ref[:, cols] = context
+        lse_ref[:, cols] = top + jnp.log2(weight_sum)
+        low = context.astype(BF16)
+        for part in range(block_q // rows):
+            send_ref[i * (block_q // rows) + part] = low[:, part * rows : (part + 1) * rows]
+        return 0
+
+    lax.fori_loop(0, length // block_q, query_step, 0)
+
+
+def attend_forward(qkv):
+    peers, _, rows = qkv.shape
+    length = peers * rows
+    block_q, block_k = 1024, 512
+    return pl.pallas_call(
+        functools.partial(forward_kernel, block_q, block_k),
+        out_shape=[
+            jax.ShapeDtypeStruct((peers, 64, rows), BF16),
+            jax.ShapeDtypeStruct((64, length), F32),
+            jax.ShapeDtypeStruct((1, length), F32),
+        ],
+        in_specs=[pl.BlockSpec(memory_space=pltpu.VMEM)],
+        out_specs=[pl.BlockSpec(memory_space=pltpu.VMEM)] * 3,
+        scratch_shapes=[
+            pltpu.VMEM((128, length), BF16),
+            pltpu.VMEM((length, 128), BF16),
+            pltpu.VMEM((80, length), BF16),
+            pltpu.VMEM((2, block_k, block_q), F32),
+        ],
+        compiler_params=pltpu.CompilerParams(vmem_limit_bytes=VMEM_LIMIT),
+        name="attend_forward",
+    )(qkv)
+
+
+def backward_kernel(
+    block_q, block_k, qkv_ref, grad_ref, context_ref, lse_ref, dq_ref, dkv_ref, qta, gta, kk, vv, kt, both, dqt
+):
+    peers, _, rows = qkv_ref.shape
+    length = peers * rows
+    row_at = lax.broadcasted_iota(jnp.int32, (16, rows), 0)
+    lane_at = lax.broadcasted_iota(jnp.int32, (rows, 16), 1)
+
+    def tail(value):
+        high, middle, low = (part.astype(F32) for part in split_three(value))
+        return jnp.where(row_at == 0, high, jnp.where(row_at == 1, middle, jnp.where(row_at == 2, low, 0.0))).astype(BF16)
+
+    minus = jnp.where(lane_at < 3, -1.0, 0.0).astype(BF16)
+    zeros = jnp.zeros((48, rows), BF16)
+
+    def prepare(j, _):
+        cols = pl.ds(pl.multiple_of(j * rows, rows), rows)
+        raw = qkv_ref[j, 0:64, :]
+        query = raw.astype(F32) * LOG2E
+        high = query.astype(BF16)
+        qta[0:64, cols] = high
+        qta[64:128, cols] = (query - high.astype(F32)).astype(BF16)
+        qta[128:144, cols] = tail(lse_ref[:, cols])
+        key = qkv_ref[j, 64:128, :]
+        kt[:, cols] = key
+        kk[cols, 0:128] = flip(jnp.concatenate([key, key], 0))
+        kk[cols, 128:144] = minus
+        grad = grad_ref[j]
+        delta = jnp.sum(grad.astype(F32) * context_ref[:, cols], 0, keepdims=True)
+        gta[0:64, cols] = grad
+        gta[64:80, cols] = tail(delta)
+        gta[80:128, cols] = zeros
+        head = (lax.broadcasted_iota(jnp.int32, (64, rows), 0) < 3).astype(F32) * -1.0
+        vv[cols, :] = flip(jnp.concatenate([qkv_ref[j, 128:192, :], head.astype(BF16)], 0))
+        both[cols, :] = flip(jnp.concatenate([raw, grad], 0))
+        return 0
+
+    lax.fori_loop(0, peers, prepare, 0)
+    dqt[...] = jnp.zeros_like(dqt)
+    first = lax.broadcasted_iota(jnp.int32, (block_k, 128), 1) < 64
+
+    def key_step(i, _):
+        here = pl.ds(pl.multiple_of(i * block_k, block_k), block_k)
+
+        def query_step(j, carry):
+            dk, dv = carry
+            cols = pl.ds(pl.multiple_of(j * block_q, block_q), block_q)
+            probs = jnp.exp2(dot32(kk[here, :], qta[:, cols]))
+            slope = dot32(vv[here, :], gta[:, cols])
+            low = (probs * slope).astype(BF16)
+            dv = dv + dot32(probs.astype(BF16), both[cols, :])
+            dk = dk + dot32(low, both[cols, :])
+            dqt[:, cols] += dot32(kt[:, here], low)
+            return dk, dv
+
+        start = jnp.zeros((block_k, 128), F32)
+        dk, dv = lax.fori_loop(0, length // block_q, query_step, (start, start))
+        dkv = jnp.where(first, dk, dv).astype(BF16)
+        for part in range(block_k // rows):
+            dkv_ref[i * (block_k // rows) + part] = dkv[part * rows : (part + 1) * rows]
+        return 0
+
+    lax.fori_loop(0, length // block_k, key_step, 0)
+
+    def finish(j, _):
+        cols = pl.ds(pl.multiple_of(j * rows, rows), rows)
+        dq_ref[j] = dqt[:, cols].astype(BF16)
+        return 0
+
+    lax.fori_loop(0, peers, finish, 0)
+
+
+def attend_backward(qkv, grad, context, lse):
+    peers, _, rows = qkv.shape
+    length = peers * rows
+    block_q, block_k = 1024, 512
+    return pl.pallas_call(
+        functools.partial(backward_kernel, block_q, block_k),
+        out_shape=[
+            jax.ShapeDtypeStruct((peers, 64, rows), BF16),
+            jax.ShapeDtypeStruct((peers, rows, 128), BF16),
+        ],
+        in_specs=[pl.BlockSpec(memory_space=pltpu.VMEM)] * 4,
+        out_specs=[pl.BlockSpec(memory_space=pltpu.VMEM)] * 2,
+        scratch_shapes=[
+            pltpu.VMEM((144, length), BF16),
+            pltpu.VMEM((128, length), BF16),
+            pltpu.VMEM((length, 144), BF16),
+            pltpu.VMEM((length, 128), BF16),
+            pltpu.VMEM((64, length), BF16),
+            pltpu.VMEM((length, 128), BF16),
+            pltpu.VMEM((64, length), F32),
+        ],
+        compiler_params=pltpu.CompilerParams(vmem_limit_bytes=VMEM_LIMIT),
+        name="attend_backward",
+    )(qkv, grad, context, lse)
+
+
+def to_owner(blocks):
+    return lax.all_to_all(blocks, "ctx", 0, 0, tiled=True)
+
+
+def heads_body(
+    tokens,
+    cotangent,
+    sequence_adapter_index,
+    query_key_value_weight,
+    output_weight,
+    first_feed_weight,
+    second_feed_weight,
+    biases,
+    value_bias_vector,
+    first_feed_bias,
+    norm_gain_pair,
+    adapter_down_factors,
+    output_down_factor,
+    adapter_up_factors,
+    hidden_up_factor,
+    hidden_down_factor,
+):
+    _, rows, width = tokens.shape
+    adapter_number = adapter_down_factors.shape[0]
+    tokens = tokens[0]
+    cotangent = cotangent[0]
+
+    def pick(table):
+        return lax.dynamic_index_in_dim(table, sequence_adapter_index[0], 0, keepdims=False)
+
+    down, out_down, up, hidden_up, hidden_down = (
+        pick(table)
+        for table in (
+            adapter_down_factors,
+            output_down_factor,
+            adapter_up_factors,
+            hidden_up_factor,
+            hidden_down_factor,
+        )
+    )
+
+    def gather(weight):
+        return lax.all_gather(weight, "fsdp", axis=0, tiled=True)
+
+    wqkv = gather(query_key_value_weight)
+    wout = gather(output_weight)
+    wfc1 = gather(first_feed_weight)
+    wfc2 = gather(second_feed_weight)
+
+    def low_sum(form, left, right):
+        return plain_sum(form, left.astype(BF16), right.astype(BF16))
+
+    projected = plain_sum("td,de->te", tokens, wqkv)
+    rank_att = plain_sum("td,jrd->jtr", tokens, down[:3])
+    lifted = low_sum("jtr,jrd->jtd", rank_att, up[:3])
+    queries = ((projected[:, :width] + biases[0] + lifted[0]) * 0.125).astype(BF16)
+    keys = (projected[:, width : 2 * width] + lifted[1]).astype(BF16)
+    values = (projected[:, 2 * width :] + value_bias_vector + lifted[2]).astype(BF16)
+    size = width // H
+    packed = (
+        jnp.stack([queries, keys, values], 0)
+        .reshape(3, rows, H, size)
+        .transpose(2, 0, 3, 1)
+        .reshape(H, 3 * size, rows)
+    )
+    qkv = to_owner(packed)
+    context_blocks, context_head, lse = attend_forward(qkv)
+    context_low = to_owner(context_blocks).reshape(width, rows).T
+    rank_out = plain_sum("td,rd->tr", context_low, out_down)
+    branch = plain_sum("td,de->te", context_low, wout) + biases[1] + low_sum("tr,rd->td", rank_out, up[3])
+
+    def first_norm(value):
+        return layer_norm(value, norm_gain_pair[0], biases[3])
+
+    def second_norm(value):
+        return layer_norm(value, norm_gain_pair[1], biases[4])
+
+    def gelu_exact(value):
+        return jax.nn.gelu(value, approximate=False)
+
+    normed, norm_back = jax.vjp(first_norm, tokens.astype(F32) + branch)
+    normed_low = normed.astype(BF16)
+    rank_fc1 = plain_sum("td,rd->tr", normed_low, down[3])
+    hidden_pre = (
+        plain_sum("td,df->tf", normed_low, wfc1) + first_feed_bias + low_sum("tr,rf->tf", rank_fc1, hidden_up)
+    )
+    activated, gelu_back = jax.vjp(gelu_exact, hidden_pre)
+    act_low = activated.astype(BF16)
+    rank_fc2 = plain_sum("tf,rf->tr", act_low, hidden_down)
+    mixed_out = plain_sum("tf,fd->td", act_low, wfc2) + biases[2] + low_sum("tr,rd->td", rank_fc2, up[4])
+    outcome, out_back = jax.vjp(second_norm, normed + mixed_out)
+    (grad_sum2,) = out_back(cotangent.astype(F32))
+    grad_mixed = grad_sum2.astype(BF16)
+    term_u2 = low_sum("tr,td->rd", rank_fc2, grad_mixed)
+    grad_rank_fc2 = plain_sum("td,rd->tr", grad_mixed, up[4]).astype(BF16)
+    term_hd = plain_sum("tr,tf->rf", grad_rank_fc2, act_low)
+    grad_act = (
+        plain_sum("td,fd->tf", grad_mixed, wfc2) + plain_sum("tr,rf->tf", grad_rank_fc2, hidden_down)
+    ).astype(BF16)
+    (grad_hidden,) = gelu_back(grad_act.astype(F32))
+    grad_hidden = grad_hidden.astype(BF16)
+    term_uh = low_sum("tr,tf->rf", rank_fc1, grad_hidden)
+    grad_rank_fc1 = plain_sum("tf,rf->tr", grad_hidden, hidden_up).astype(BF16)
+    term_d1 = plain_sum("tr,td->rd", grad_rank_fc1, normed_low)
+    grad_normed_low = (
+        plain_sum("tf,df->td", grad_hidden, wfc1) + plain_sum("tr,rd->td", grad_rank_fc1, down[3])
+    ).astype(BF16)
+    (grad_resid,) = norm_back(grad_sum2 + grad_normed_low.astype(F32))
+    grad_branch = grad_resid.astype(BF16)
+    term_uo = low_sum("tr,td->rd", rank_out, grad_branch)
+    grad_rank_out = plain_sum("td,rd->tr", grad_branch, up[3]).astype(BF16)
+    term_do = plain_sum("tr,td->rd", grad_rank_out, context_low)
+    grad_context = (
+        plain_sum("td,ed->te", grad_branch, wout) + plain_sum("tr,rd->td", grad_rank_out, out_down)
+    ).astype(BF16)
+    grad_blocks = to_owner(grad_context.reshape(rows, H, size).transpose(1, 2, 0))
+    dq_blocks, dkv_blocks = attend_backward(qkv, grad_blocks, context_head, lse)
+    grad_qlin = to_owner(dq_blocks).reshape(width, rows).T * jnp.asarray(0.125, BF16)
+    dkv = to_owner(dkv_blocks).reshape(H, rows, 2, size).transpose(2, 1, 0, 3).reshape(2, rows, width)
+    joined = jnp.concatenate([grad_qlin, dkv[0], dkv[1]], -1)
+    stacked = joined.reshape(rows, 3, width).swapaxes(0, 1)
+    term_up = low_sum("jtr,jtd->jrd", rank_att, stacked)
+    grad_rank_att = plain_sum("jtd,jrd->jtr", stacked, up[:3]).astype(BF16)
+    term_down = plain_sum("jtr,td->jrd", grad_rank_att, tokens)
+    grad_tokens = (
+        grad_resid
+        + plain_sum("te,de->td", joined, wqkv)
+        + plain_sum("jtr,jrd->td", grad_rank_att, down[:3])
+    )
+    mine = (
+        jnp.concatenate([term_down, term_d1[None]], 0),
+        term_do,
+        jnp.concatenate([term_up, term_uo[None], term_u2[None]], 0),
+        term_uh,
+        term_hd,
+    )
+    summed = lax.psum(mine, "ctx")
+    index_all = lax.all_gather(sequence_adapter_index, "fsdp", axis=0, tiled=True)
+    picker = index_all[:, None] == jnp.arange(adapter_number, dtype=jnp.int32)[None, :]
+
+    def to_table(total):
+        every = lax.all_gather(total, "fsdp", axis=0)
+        table = 0.0
+        for seq in range(every.shape[0]):
+            mask = picker[seq].reshape((adapter_number,) + (1,) * total.ndim)
+            table = table + jnp.where(mask, every[seq][None], 0.0)
+        return table
+
+    tables = [to_table(total) for total in summed]
+    return (outcome.astype(BF16)[None], grad_tokens[None], *tables)
+
+
 def solution(mesh):
+    one_head_each = mesh.shape["ctx"] == H
     return jax.shard_map(
-        body,
+        heads_body if one_head_each else gather_body,
         mesh=mesh,
         in_specs=(
             P("fsdp", "ctx", None),

time: 1090 us -> 451 us (0.41)
  waiting for transfers between devices: 697 us -> 181 us
  matrix products: 247 us -> 78.2 us
  Pallas kernels: 0 us -> 78.3 us
  local copies, waits for them, and re-layouts: 81.7 us -> 13.4 us
  blocking collectives: 0 us -> 50.2 us
  starting transfers between devices: 0.64 us -> 19.8 us
  other arithmetic: 30.3 us -> 13.7 us
  loops' own time: 11.6 us -> 0 us
    reduce_scatter x2 -> x0, waiting for transfers between devices: 330 us -> none  [the longest x1 183 us: body(): lax.psum_scatter(grad_key_all.reshape(seq_count, length, model_width).ast...]
    all_gather x6 -> x4, waiting for transfers between devices: 175 us -> 15 us  [gather(): return lax.all_gather(weight, 'fsdp', axis=0, tiled=True)]
    dot_general x76 -> x32, matrix products: 204 us -> 78.2 us  [plain_sum(): return jnp.einsum(form, left, right, preferred_element_type=jnp.float32)]
    psum x1, waiting for transfers between devices: 189 us -> 107 us  [heads_body(): summed = lax.psum(mine, 'ctx')]
    pallas_call x0 -> x2, Pallas kernels: none -> 78.3 us  [the longest x1 51.9 us: attend_backward(): pl.pallas_call(functools.partial(backward_kernel, block_q, block_k), out_...]
    all_to_all x0 -> x3, waiting for transfers between devices: none -> 56.2 us  [to_owner(): return lax.all_to_all(blocks, 'ctx', 0, 0, tiled=True)]
    dot_general x17 -> x0, matrix products: 42.4 us -> none  [the longest x12 31.9 us: exact_sum(): jnp.einsum(form, left, right, precision=HIGHEST, preferred_element_type=j...]
    all_to_all x0 -> x2, blocking collectives: none -> 36.4 us  [to_owner(): return lax.all_to_all(blocks, 'ctx', 0, 0, tiled=True)]
  transfers between devices with their start and end apart: 9 -> 8, of which waited for: 6 -> 5; matrix products, arithmetic and copies ran while one was open for 17% -> 13% of each run, Pallas kernels for 0% -> 6%
where the time goes in v1:
time: 451 us; the launch traced here: 450 us
  waiting for transfers between devices  181 us (40%)
  Pallas kernels  78.3 us (17%)
  matrix products  78.2 us (17%)
  blocking collectives  50.2 us (11%)
  starting transfers between devices  19.8 us (4%)
  between operations  15.1 us (3%)
  other arithmetic  13.7 us (3%)
  local copies, waits for them, and re-layouts  13.4 us (3%)
    psum x1, waiting for transfers between devices, heads_body(): summed = lax.psum(mine, 'ctx')  107 us
    dot_general x32, matrix products, plain_sum(): return jnp.einsum(form, left, right, preferred_element_type=jnp.float32)  78.2 us
    all_to_all x3, waiting for transfers between devices, to_owner(): return lax.all_to_all(blocks, 'ctx', 0, 0, tiled=True)  56.2 us
    pallas_call x1, Pallas kernels, attend_backward(): pl.pallas_call(functools.partial(backward_kernel, block_q, block_k), out_...  51.9 us
    all_to_all x2, blocking collectives, to_owner(): return lax.all_to_all(blocks, 'ctx', 0, 0, tiled=True)  36.4 us
    pallas_call x1, Pallas kernels, attend_forward(): pl.pallas_call(functools.partial(forward_kernel, block_q, block_k), out_s...  26.4 us
    all_to_all x3, starting transfers between devices, to_owner(): return lax.all_to_all(blocks, 'ctx', 0, 0, tiled=True)  19.6 us
    all_gather x4, waiting for transfers between devices, gather(): return lax.all_gather(weight, 'fsdp', axis=0, tiled=True)  15 us
  transfers between devices with their start and end apart: 8, of which 5 were waited for; matrix products, arithmetic and copies ran while one was open for 13% of the time, Pallas kernels for 6%

profile of v1, /device:TPU:0, one launch (start us, length us, event | category | flops | bytes accessed | tf_op | source)
XLA Modules:
  0.0 450.0 jit_solution(12172787092879078434)
XLA Ops:
  11.9 2.2 fusion.58
  14.1 14.9 %all-gather.5.cloned.1.call-done = bf16[1024,3072]{1,0:T(8,128)(2,1)} async-done(((bf16[512,3072]{1,0:T(8,128)(2,1)}), bf16[1024,3072]{1,0:T(8,128)(2,1)}) %all-gather.5.cloned.1.call-update) | async-done | bytes 6291472 | tf_op jit(solution)/shard_map/all_gather | solution.py:551
  29.1 4.7 %fusion.48 = f32[256,3072]{1,0:T(8,128)S(1)} fusion(bf16[1024,3072]{1,0:T(8,128)(2,1)} %all-gather.5.cloned.1.call-done, bf16[1,256,1024]{2,1,0:T(8,128)(2,1)S(1)} %copy-done.11), kind=kOutput, calls=%fused_computation.103 | convolution fusion | flops 1610612736 | bytes 9961472 | tf_op jit(solution)/shard_map/td,de->te/dot_general | solution.py:22
  36.1 1.2 maximum_bitcast_fusion
  37.3 1.2 copy.46
  38.5 6.8 %all-to-all-start = ((bf16[16,192,256]{2,1,0:T(8,128)(2,1)}), bf16[16,192,256]{2,1,0:T(8,128)(2,1)S(1)}, u32[]{:S(2)}, u32[]{:S(2)}) async-start(bf16[16,192,256]{2,1,0:T(8,128)(2,1)} %bitcast.209), calls=%async_computation | async-start | bytes 3145728 | tf_op jit(solution)/shard_map/all_to_all | solution.py:510
  45.9 33.7 %all-to-all-done.qkv_ref = bf16[16,192,256]{2,1,0:T(8,128)(2,1)S(1)} async-done(((bf16[16,192,256]{2,1,0:T(8,128)(2,1)}), bf16[16,192,256]{2,1,0:T(8,128)(2,1)S(1)}, u32[]{:S(2)}, u32[]{:S(2)}) %all-to-all-start) | async-done | bytes 1572896 | tf_op jit(solution)/shard_map/all_to_all | solution.py:510
  80.7 26.4 %attend_forward.1 = (bf16[16,64,256]{2,1,0:T(8,128)(2,1)}, f32[64,4096]{1,0:T(8,128)}, f32[1,4096]{1,0:T(1,128)}) custom-call(bf16[16,192,256]{2,1,0:T(8,128)(2,1)} %copy-done.1), custom_call_target="tpu_custom_call" | custom-call | tf_op jit(solution)/shard_map/attend_forward/pallas_call | solution.py:391
  107.1 8.4 %all-to-all-start.1 = ((bf16[16,64,256]{2,1,0:T(8,128)(2,1)}), bf16[16,64,256]{2,1,0:T(8,128)(2,1)S(1)}, u32[]{:S(2)}, u32[]{:S(2)}) async-start(bf16[16,64,256]{2,1,0:T(8,128)(2,1)} %get-tuple-element.12), calls=%async_computation.1 | async-start | bytes 1048576 | tf_op jit(solution)/shard_map/all_to_all | solution.py:510
  115.6 14.5 %all-to-all-done.1 = bf16[16,64,256]{2,1,0:T(8,128)(2,1)S(1)} async-done(((bf16[16,64,256]{2,1,0:T(8,128)(2,1)}), bf16[16,64,256]{2,1,0:T(8,128)(2,1)S(1)}, u32[]{:S(2)}, u32[]{:S(2)}) %all-to-all-start.1) | async-done | bytes 524320 | tf_op jit(solution)/shard_map/all_to_all | solution.py:510
  131.1 2.3 convolution_add_fusion.7
  135.4 5.7 %convolution_add_fusion.2 = f32[256,4096]{1,0:T(8,128)S(1)} fusion(bf16[256,1024]{1,0:T(8,128)(2,1)S(1)} %fusion.42, bf16[1024,4096]{1,0:T(8,128)(2,1)} %all-gather.9.cloned.1.call-done, f32[4096]{0:T(1024)S(1)} %copy-done.34), kind=kOutput, calls=%fused_computation.5 | convolution fusion | flops 2148532224 | bytes 13123584 | tf_op jit(solution)/shard_map/td,df->tf/dot_general | solution.py:22
  141.2 12.3 %multiply_convert_fusion = (bf16[256,4096]{1,0:T(8,128)(2,1)S(1)}, f32[256,4096]{1,0:T(8,128)}, f32[256,4096]{1,0:T(8,128)}) fusion(f32[256,4096]{1,0:T(8,128)S(1)} %convolution_add_fusion.2, bf16[256,16]{0,1:T(8,128)(2,1)S(1)} %convolution_convert_fusion.7, bf16[8,16,4096]{2,1,0:T(8,128)(2,1)} %param.30, s32[]{:T(128)S(6)} %select_n.45), kind=kOutput, calls=%fused_computation.17 | convolution fusion | flops 102760448 | bytes 14819332 | tf_op jit(solution)/shard_map/tr,rf->tf/dot_general | solution.py:22
  153.4 1.3 copy-done.4
  154.8 1.5 convolution_convert_fusion.3
  156.3 6.5 %convolution_add_fusion.8 = f32[256,1024]{1,0:T(8,128)S(1)} fusion(bf16[256,4096]{1,0:T(8,128)(2,1)} %copy-done.4, bf16[4096,1024]{1,0:T(8,128)(2,1)} %all-gather.11.cloned.1.call-done, f32[1024]{0:T(1024)S(1)} %bitcast.233), kind=kOutput, calls=%fused_computation.56 | convolution fusion | flops 2147745792 | bytes 11538432 | tf_op jit(solution)/shard_map/tf,fd->td/dot_general | solution.py:22
  163.8 1.3 fusion.85
  165.5 4.4 fusion.92
  169.9 5.8 %fusion.6 = bf16[256,4096]{1,0:T(8,128)(2,1)S(1)} fusion(f32[256,4096]{1,0:T(8,128)} %get-tuple-element.29, f32[256,4096]{1,0:T(8,128)} %fusion.92, bf16[256,16]{0,1:T(8,128)(2,1)S(1)} %convolution_convert_fusion.6, f32[256,4096]{1,0:T(8,128)} %get-tuple-element.61, bf16[8,16,4096]{2,1,0:T(8,128)(2,1)} %param.31, s32[]{:T(128)S(6)} %select_n.45), kind=kOutput, calls=%fused_computation.14 | convolution fusion | flops 51380224 | bytes 14819332 | tf_op jit(solution)/shard_map/tr,rf->tf/dot_general | solution.py:22
  175.8 1.7 convolution_convert_fusion.2
  177.5 2.4 fusion.93
  179.9 1.5 multiply_reduce_fusion
  185.1 18.2 %all_to_all.25.grad_ref = bf16[16,64,256]{2,1,0:T(8,128)(2,1)} all-to-all(bf16[16,64,256]{2,1,0:T(8,128)(2,1)S(1)} %bitcast.215), channel_id=1, replica_groups=mesh['ctx'=16,'fsdp'=2] {'ctx'}, dimensions={0} | all-to-all | bytes 1048576 | tf_op jit(solution)/shard_map/all_to_all | solution.py:510
  203.3 51.9 %attend_backward.1 = (bf16[16,64,256]{2,1,0:T(8,128)(2,1)}, bf16[16,256,128]{2,1,0:T(8,128)(2,1)}) custom-call(bf16[16,192,256]{2,1,0:T(8,128)(2,1)} %copy-done.1, bf16[16,64,256]{2,1,0:T(8,128)(2,1)} %all_to_all.25.grad_ref, f32[64,4096]{1,0:T(8,128)} %get-tuple-element.13.context_ref, f32[1,4096]{1,0:T(1,128)} %get-tuple-element.14.lse_ref), custom_call_target="tpu_custom_call" | custom-call | tf_op jit(solution)/shard_map/attend_backward/pallas_call | solution.py:487
  255.2 18.2 %all_to_all.26 = bf16[16,64,256]{2,1,0:T(8,128)(2,1)} all-to-all(bf16[16,64,256]{2,1,0:T(8,128)(2,1)} %get-tuple-element.15), channel_id=1, replica_groups=mesh['ctx'=16,'fsdp'=2] {'ctx'}, dimensions={0} | all-to-all | bytes 1048576 | tf_op jit(solution)/shard_map/all_to_all | solution.py:510
  273.4 4.4 all-to-all-start.4
  279.2 2.4 all-reduce
  281.5 1.4 convolution_bitcast_fusion.4
  282.9 1.2 convolution_bitcast_fusion.3
  284.1 1.9 convolution_bitcast_fusion.5
  286.1 1.8 convolution_bitcast_fusion.6
  287.9 1.8 convolution_bitcast_fusion
  289.7 1.8 convolution_bitcast_fusion.1
  292.6 8.0 %all-to-all-done.4 = bf16[16,256,128]{2,1,0:T(8,128)(2,1)} async-done(((bf16[16,256,128]{2,1,0:T(8,128)(2,1)}), bf16[16,256,128]{2,1,0:T(8,128)(2,1)}, u32[]{:S(2)}, u32[]{:S(2)}) %all-to-all-start.4) | async-done | bytes 1048608 | tf_op jit(solution)/shard_map/all_to_all | solution.py:510
  300.6 1.5 copy.49
  303.4 1.4 fusion.43
  304.9 2.0 convolution_convert_fusion
  309.9 5.0 %fusion.24 = f32[256,1024]{1,0:T(8,128)S(1)} fusion(bf16[1024,3072]{1,0:T(8,128)(2,1)} %all-gather.5.cloned.1.call-done, bf16[256,1024]{1,0:T(8,128)(2,1)S(1)} %copy.51, bf16[256,1024]{1,0:T(8,128)(2,1)} %copy.50, bf16[256,1024]{1,0:T(8,128)(2,1)} %bitcast.222, f32[256,1024]{1,0:T(8,128)S(1)} %copy-done.15, f32[256]{0:T(256)S(1)} %copy-done.33), kind=kOutput, calls=%fused_computation.55 | convolution fusion | flops 1615855616 | bytes 9962496 | tf_op jit(solution)/shard_map/te,de->td/dot_general | solution.py:22
  314.9 2.2 fusion.23
  317.1 107.5 %all-reduce.4.cloned.1.call-done = (f32[1,4,16,1024]{3,2,1,0:T(8,128)}, f32[1,16,1024]{2,1,0:T(8,128)}, f32[1,5,16,1024]{3,2,1,0:T(8,128)}, f32[1,16,4096]{2,1,0:T(8,128)}, f32[1,16,4096]{2,1,0:T(8,128)}) async-done(((f32[1,4,16,1024]{3,2,1,0:T(8,128)}, f32[1,16,1024]{2,1,0:T(8,128)}, f32[1,5,16,1024]{3,2,1,0:T(8,128)}, f32[1,16,4096]{2,1,0:T(8,128)}, f32[1,16,4096]{2,1,0:T(8,128)}), ...) | async-done | bytes 1179664 | tf_op jit(solution)/shard_map/psum | solution.py:645
  424.5 2.5 all_gather.59
  427.1 2.4 all_gather.57
  429.5 2.5 all_gather.55
  432.1 1.9 all_gather.53
  434.0 2.2 all_gather.51
  436.2 1.9 select_add_fusion
  439.1 1.7 select_add_fusion.3
  440.8 2.7 select_add_fusion.1
  (146 shorter events, 23.7 us)
Async XLA Ops:
  7.2 4.7 %copy-start = (bf16[8,5,16,1024]{3,2,1,0:T(8,128)(2,1)S(1)}, bf16[8,5,16,1024]{3,2,1,0:T(8,128)(2,1)}, u32[]{:S(2)}) copy-start(bf16[8,5,16,1024]{3,2,1,0:T(8,128)(2,1)} %param.29) | copy-start | bytes 3932164
  7.2 2.9 copy-start.29
  7.2 2.9 copy-start.11
  7.2 21.9 %all-gather.5.cloned.1.call-start = ((), (), s32[]{:S(2)}) async-start(), calls=%async_computation.5 | async-start | bytes 9437184 | tf_op jit(solution)/shard_map/all_gather | solution.py:551
  7.9 123.1 %all-gather.7.cloned.1.call-start = ((), (), s32[]{:S(2)}) async-start(), calls=%async_computation.6 | async-start | bytes 3145728 | tf_op jit(solution)/shard_map/all_gather | solution.py:551
  8.7 126.7 %all-gather.9.cloned.1.call-start = ((), (), s32[]{:S(2)}) async-start(), calls=%async_computation.7 | async-start | bytes 12582912 | tf_op jit(solution)/shard_map/all_gather | solution.py:551
  11.3 0.6 copy-start.22
  14.1 19.7 %copy-start.31 = (f32[1024]{0:T(1024)S(1)}, f32[1024]{0:T(1024)}, u32[]{:S(2)}) copy-start(f32[1024]{0:T(1024)} %param.24) | copy-start | bytes 12292
  29.1 4.7 %copy-start.2 = (f32[3,256,1024]{2,1,0:T(8,128)S(1)}, f32[3,256,1024]{2,1,0:T(8,128)}, u32[]{:S(2)}) copy-start(f32[3,256,1024]{2,1,0:T(8,128)} %fusion.58) | copy-start | bytes 9437188
  38.5 41.0 %all-to-all-start = ((bf16[16,192,256]{2,1,0:T(8,128)(2,1)}), bf16[16,192,256]{2,1,0:T(8,128)(2,1)S(1)}, u32[]{:S(2)}, u32[]{:S(2)}) async-start(bf16[16,192,256]{2,1,0:T(8,128)(2,1)} %bitcast.209), calls=%async_computation | async-start | bytes 3145728 | tf_op jit(solution)/shard_map/all_to_all | solution.py:510
  45.3 70.3 %copy-start.30 = (f32[2,1024]{1,0:T(2,128)S(1)}, f32[2,1024]{1,0:T(2,128)}, u32[]{:S(2)}) copy-start(f32[2,1024]{1,0:T(2,128)} %param.26) | copy-start | bytes 24580
  45.3 111.0 %all-gather.11.cloned.1.call-start = ((), (), s32[]{:S(2)}) async-start(), calls=%async_computation.8 | async-start | bytes 12582912 | tf_op jit(solution)/shard_map/all_gather | solution.py:551
  79.6 1.1 copy-start.1
  107.1 23.0 %all-to-all-start.1 = ((bf16[16,64,256]{2,1,0:T(8,128)(2,1)}), bf16[16,64,256]{2,1,0:T(8,128)(2,1)S(1)}, u32[]{:S(2)}, u32[]{:S(2)}) async-start(bf16[16,64,256]{2,1,0:T(8,128)(2,1)} %get-tuple-element.12), calls=%async_computation.1 | async-start | bytes 1048576 | tf_op jit(solution)/shard_map/all_to_all | solution.py:510
  130.1 0.9 copy-start.8
  131.1 4.4 copy-start.34
  134.3 6.8 %copy-start.10 = (bf16[256,1024]{1,0:T(8,128)(2,1)}, bf16[256,1024]{1,0:T(8,128)(2,1)S(1)}, u32[]{:S(2)}) copy-start(bf16[256,1024]{1,0:T(8,128)(2,1)S(1)} %fusion.42) | copy-start | bytes 1572868
  135.4 5.8 %copy-start.27 = (bf16[256,16]{0,1:T(8,128)(2,1)}, bf16[256,16]{0,1:T(8,128)(2,1)S(1)}, u32[]{:S(2)}) copy-start(bf16[256,16]{0,1:T(8,128)(2,1)S(1)} %convolution_convert_fusion.7) | copy-start | bytes 24580
  153.4 1.3 copy-start.4
  156.3 9.1 %slice-start.2 = ((s8[8388608]{0:T(1024)(128)(4,1)}), s8[4194304]{0:T(1024)(128)(4,1)S(1)}, s32[]{:S(2)}) async-start(s8[8388608]{0:T(1024)(128)(4,1)} %bitcast.236), calls=%async_computation.12 | async-start | bytes 8388608
  156.3 7.1 %copy-start.17 = (bf16[1,256,1024]{2,1,0:T(8,128)(2,1)S(1)}, bf16[1,256,1024]{2,1,0:T(8,128)(2,1)}, u32[]{:S(2)}) copy-start(bf16[1,256,1024]{2,1,0:T(8,128)(2,1)} %param.17) | copy-start | bytes 1572868
  156.3 9.1 %slice-start.3 = ((s8[8388608]{0:T(1024)(128)(4,1)}), s8[4194304]{0:T(1024)(128)(4,1)S(1)}, s32[]{:S(2)}) async-start(s8[8388608]{0:T(1024)(128)(4,1)} %bitcast.236), calls=%async_computation.13 | async-start | bytes 8388608
  165.1 12.4 %slice-start = ((s8[8388608]{0:T(1024)(128)(4,1)}), s8[4194304]{0:T(1024)(128)(4,1)S(1)}, s32[]{:S(2)}) async-start(s8[8388608]{0:T(1024)(128)(4,1)} %bitcast.234), calls=%async_computation.10 | async-start | bytes 8388608
  165.2 4.7 %copy-start.13 = (bf16[256,1024]{1,0:T(8,128)(2,1)}, bf16[256,1024]{1,0:T(8,128)(2,1)S(1)}, u32[]{:S(2)}) copy-start(bf16[256,1024]{1,0:T(8,128)(2,1)S(1)} %add_convert_fusion.2) | copy-start | bytes 1572868
  165.5 4.5 copy-start.28
  165.5 12.0 %slice-start.1 = ((s8[8388608]{0:T(1024)(128)(4,1)}), s8[4194304]{0:T(1024)(128)(4,1)S(1)}, s32[]{:S(2)}) async-start(s8[8388608]{0:T(1024)(128)(4,1)} %bitcast.234), calls=%async_computation.11 | async-start | bytes 8388608
  175.8 4.1 copy-start.6
  179.9 3.1 copy-start.3
  181.8 1.0 copy-start.14
  182.8 1.0 copy-start.9
  183.0 72.2 %copy-start.25 = (bf16[256,16]{0,1:T(8,128)(2,1)}, bf16[256,16]{0,1:T(8,128)(2,1)S(1)}, u32[]{:S(2)}) copy-start(bf16[256,16]{0,1:T(8,128)(2,1)S(1)} %convolution_convert_fusion.5) | copy-start | bytes 24580
  184.9 92.9 %copy-start.35 = (u32[32]{0:T(128)S(1)}, u32[32]{0:T(128)}, u32[]{:S(2)}) copy-start(u32[32]{0:T(128)} %constant.106) | copy-start | bytes 388
  203.3 84.6 %copy-start.5 = (bf16[256,4096]{1,0:T(8,128)(2,1)S(1)}, bf16[256,4096]{1,0:T(8,128)(2,1)}, u32[]{:S(2)}) copy-start(bf16[256,4096]{1,0:T(8,128)(2,1)} %copy-done.4) | copy-start | bytes 6291460
  273.4 27.2 %all-to-all-start.4 = ((bf16[16,256,128]{2,1,0:T(8,128)(2,1)}), bf16[16,256,128]{2,1,0:T(8,128)(2,1)}, u32[]{:S(2)}, u32[]{:S(2)}) async-start(bf16[16,256,128]{2,1,0:T(8,128)(2,1)} %get-tuple-element.16), calls=%async_computation.4 | async-start | bytes 2097152 | tf_op jit(solution)/shard_map/all_to_all | solution.py:510
  277.8 146.8 %all-reduce.4.cloned.1.call-start = ((), (), s32[]{:S(2)}) async-start(), calls=%async_computation.9 | async-start | bytes 2359296 | tf_op jit(solution)/shard_map/psum | solution.py:645
  281.5 8.2 %copy-start.7 = (bf16[256,4096]{1,0:T(8,128)(2,1)S(1)}, bf16[256,4096]{1,0:T(8,128)(2,1)}, u32[]{:S(2)}) copy-start(bf16[256,4096]{1,0:T(8,128)(2,1)} %copy-done.6) | copy-start | bytes 6291460
  281.5 10.0 %copy-start.16 = (bf16[16,64,256]{2,1,0:T(8,128)(2,1)S(1)}, bf16[16,64,256]{2,1,0:T(8,128)(2,1)}, u32[]{:S(2)}) copy-start(bf16[16,64,256]{2,1,0:T(8,128)(2,1)} %all_to_all.26) | copy-start | bytes 1572868
  302.4 0.8 copy-start.18
  302.6 0.8 copy-start.19
  302.6 4.2 copy-start.12
  303.4 3.6 copy-start.21
  304.9 3.7 copy-start.36
  304.9 5.0 %copy-start.15 = (f32[256,1024]{1,0:T(8,128)S(1)}, f32[256,1024]{1,0:T(8,128)}, u32[]{:S(2)}) copy-start(f32[256,1024]{1,0:T(8,128)} %copy-done.14) | copy-start | bytes 3145732
  304.9 5.0 %copy-start.33 = (f32[256]{0:T(256)S(1)}, f32[256]{0:T(256)}, u32[]{:S(2)}) copy-start(f32[256]{0:T(256)} %copy-done.32) | copy-start | bytes 3076
  306.8 1.0 copy-start.23
  309.9 5.0 %copy-start.24 = (bf16[3,256,16]{1,2,0:T(8,128)(2,1)S(1)}, bf16[3,256,16]{1,2,0:T(8,128)(2,1)}, u32[]{:S(2)}) copy-start(bf16[3,256,16]{1,2,0:T(8,128)(2,1)} %copy-done.23) | copy-start | bytes 73732
  424.5 7.5 %copy-start.26 = (f32[1,16,1024]{2,1,0:T(8,128)S(1)}, f32[1,16,1024]{2,1,0:T(8,128)}, u32[]{:S(2)}) copy-start(f32[1,16,1024]{2,1,0:T(8,128)} %get-tuple-element.20) | copy-start | bytes 196612
  424.5 9.4 %copy-start.20 = (f32[1,4,16,1024]{3,2,1,0:T(8,128)S(1)}, f32[1,4,16,1024]{3,2,1,0:T(8,128)}, u32[]{:S(2)}) copy-start(f32[1,4,16,1024]{3,2,1,0:T(8,128)} %get-tuple-element.19) | copy-start | bytes 786436
  (1 other events, 0.6 us)
Sparse Core Ops, SparseCore 0:
  9.6 19.4 all-gather.4
  30.6 11.7 all-gather.6
  43.9 21.0 all-gather.8
  66.4 21.0 all-gather.10
  308.7 115.8 all-reduce.3

commit v2 on v1

--- a/solution.py
+++ b/solution.py
@@ -315,6 +315,7 @@
 F32 = jnp.float32
 LOG2E = 1.4426950408889634
 VMEM_LIMIT = 56 * 2**20
+MESH = pl.DeviceIdType.MESH
 
 
 def dot32(left, right):
@@ -504,6 +505,79 @@
         compiler_params=pltpu.CompilerParams(vmem_limit_bytes=VMEM_LIMIT),
         name="attend_backward",
     )(qkv, grad, context, lse)
+
+
+def reduce_kernel(mine_ref, out_ref, parts, send_one, recv_one, send_two, recv_two, send_last, recv_last):
+    peers = mine_ref.shape[0]
+    me = lax.axis_index("ctx")
+    core = lax.axis_index("fsdp")
+    barrier = pltpu.get_barrier_semaphore()
+    for step in range(1, peers):
+        pl.semaphore_signal(barrier, inc=1, device_id=(me ^ step, core), device_id_type=MESH)
+    pl.semaphore_signal(barrier, inc=1, device_id=(me, 1 - core), device_id_type=MESH)
+    pl.semaphore_wait(barrier, peers)
+    scatter = [
+        pltpu.make_async_remote_copy(
+            src_ref=mine_ref.at[me ^ step],
+            dst_ref=parts.at[step],
+            send_sem=send_one.at[step],
+            recv_sem=recv_one.at[step],
+            device_id=(me ^ step, core),
+            device_id_type=MESH,
+        )
+        for step in range(1, peers)
+    ]
+    for copy in scatter:
+        copy.start()
+    total = mine_ref[me].astype(F32)
+    for step in range(1, peers):
+        scatter[step - 1].wait_recv()
+        total = total + parts[step].astype(F32)
+    out_ref[core, me] = total.astype(BF16)
+    gather = [
+        pltpu.make_async_remote_copy(
+            src_ref=out_ref.at[core, me],
+            dst_ref=out_ref.at[core, me],
+            send_sem=send_two.at[step],
+            recv_sem=recv_two.at[step],
+            device_id=(me ^ step, core),
+            device_id_type=MESH,
+        )
+        for step in range(1, peers)
+    ]
+    for copy in gather:
+        copy.start()
+    for copy in gather:
+        copy.wait_recv()
+    last = pltpu.make_async_remote_copy(
+        src_ref=out_ref.at[core],
+        dst_ref=out_ref.at[core],
+        send_sem=send_last,
+        recv_sem=recv_last,
+        device_id=(me, 1 - core),
+        device_id_type=MESH,
+    )
+    last.start()
+    for copy in scatter + gather:
+        copy.wait_send()
+    last.wait()
+
+
+def reduce_terms(mine, collective_id):
+    peers, rows, lanes = mine.shape
+    return pl.pallas_call(
+        reduce_kernel,
+        out_shape=jax.ShapeDtypeStruct((2, peers, rows, lanes), BF16),
+        in_specs=[pl.BlockSpec(memory_space=pltpu.VMEM)],
+        out_specs=pl.BlockSpec(memory_space=pltpu.VMEM),
+        scratch_shapes=[pltpu.VMEM((peers, rows, lanes), BF16)]
+        + [pltpu.SemaphoreType.DMA((peers,))] * 4
+        + [pltpu.SemaphoreType.DMA] * 2,
+        compiler_params=pltpu.CompilerParams(
+            collective_id=collective_id, has_side_effects=True, vmem_limit_bytes=VMEM_LIMIT
+        ),
+        name="reduce_terms",
+    )(mine)
 
 
 def to_owner(blocks):
@@ -642,24 +716,26 @@
         term_uh,
         term_hd,
     )
-    summed = lax.psum(mine, "ctx")
+    flat = jnp.concatenate([term.reshape(-1, 128) for term in mine], 0)
+    summed = reduce_terms(flat.astype(BF16).reshape(H, -1, 128), 0).reshape(2, -1, 128)
     index_all = lax.all_gather(sequence_adapter_index, "fsdp", axis=0, tiled=True)
     picker = index_all[:, None] == jnp.arange(adapter_number, dtype=jnp.int32)[None, :]
-
-    def to_table(total):
-        every = lax.all_gather(total, "fsdp", axis=0)
+    tables = []
+    at = 0
+    for term in mine:
+        count = term.size // 128
+        every = summed[:, at : at + count].reshape((2,) + term.shape).astype(F32)
+        at += count
         table = 0.0
-        for seq in range(every.shape[0]):
-            mask = picker[seq].reshape((adapter_number,) + (1,) * total.ndim)
+        for seq in range(2):
+            mask = picker[seq].reshape((adapter_number,) + (1,) * term.ndim)
             table = table + jnp.where(mask, every[seq][None], 0.0)
-        return table
-
-    tables = [to_table(total) for total in summed]
+        tables.append(table)
     return (outcome.astype(BF16)[None], grad_tokens[None], *tables)
 
 
 def solution(mesh):
-    one_head_each = mesh.shape["ctx"] == H
+    one_head_each = mesh.shape["ctx"] == H and mesh.shape["fsdp"] == 2
     return jax.shard_map(
         heads_body if one_head_each else gather_body,
         mesh=mesh,

time: 451 us -> 398 us (0.88)
  waiting for transfers between devices: 181 us -> 74.2 us
  Pallas kernels: 78.3 us -> 115 us
  local copies, waits for them, and re-layouts: 13.4 us -> 39.4 us
  blocking collectives: 50.2 us -> 38 us
    psum x1 -> x0, waiting for transfers between devices: 107 us -> none  [heads_body(): summed = lax.psum(mine, 'ctx')]
    pallas_call x0 -> x1, Pallas kernels: none -> 36.5 us  [reduce_terms(): pl.pallas_call(reduce_kernel, out_shape=jax.ShapeDtypeStruct((2, peers, r...]
    broadcast_in_dim x6 -> x11, local copies, waits for them, and re-layouts: 0.17 us -> 14.4 us  [heads_body(): table = table + jnp.where(mask, every[seq][None], 0.0)]
    all_gather x5 -> x0, blocking collectives: 11.5 us -> none  [to_table(): every = lax.all_gather(total, 'fsdp', axis=0)]
  transfers between devices with their start and end apart: 8 -> 7, of which waited for: 5 -> 4; matrix products, arithmetic and copies ran while one was open for 13% -> 13% of each run, Pallas kernels for 6% -> 7%
where the time goes in v2:
time: 398 us; the launch traced here: 396 us
  Pallas kernels  115 us (29%)
  matrix products  77.9 us (20%)
  waiting for transfers between devices  74.2 us (19%)
  local copies, waits for them, and re-layouts  39.4 us (10%)
  blocking collectives  38 us (10%)
  starting transfers between devices  19.9 us (5%)
  other arithmetic  16.7 us (4%)
  between operations  15.1 us (4%)
    dot_general x32, matrix products, plain_sum(): return jnp.einsum(form, left, right, preferred_element_type=jnp.float32)  77.9 us
    all_to_all x3, waiting for transfers between devices, to_owner(): return lax.all_to_all(blocks, 'ctx', 0, 0, tiled=True)  56.6 us
    pallas_call x1, Pallas kernels, attend_backward(): pl.pallas_call(functools.partial(backward_kernel, block_q, block_k), out_...  51.7 us
    pallas_call x1, Pallas kernels, reduce_terms(): pl.pallas_call(reduce_kernel, out_shape=jax.ShapeDtypeStruct((2, peers, r...  36.5 us
    all_to_all x2, blocking collectives, to_owner(): return lax.all_to_all(blocks, 'ctx', 0, 0, tiled=True)  36.2 us
    pallas_call x1, Pallas kernels, attend_forward(): pl.pallas_call(functools.partial(forward_kernel, block_q, block_k), out_s...  26.4 us
    all_to_all x3, starting transfers between devices, to_owner(): return lax.all_to_all(blocks, 'ctx', 0, 0, tiled=True)  19.7 us
    all_gather x4, waiting for transfers between devices, gather(): return lax.all_gather(weight, 'fsdp', axis=0, tiled=True)  14.9 us
  transfers between devices with their start and end apart: 7, of which 4 were waited for; matrix products, arithmetic and copies ran while one was open for 13% of the time, Pallas kernels for 7%

profile of v2, /device:TPU:0, one launch (start us, length us, event | category | flops | bytes accessed | tf_op | source)
XLA Modules:
  0.0 395.8 jit_solution(6565742525733870052)
XLA Ops:
  11.9 2.2 fusion.59
  14.1 14.9 %all-gather.5.cloned.1.call-done = bf16[1024,3072]{1,0:T(8,128)(2,1)} async-done(((bf16[512,3072]{1,0:T(8,128)(2,1)}), bf16[1024,3072]{1,0:T(8,128)(2,1)}) %all-gather.5.cloned.1.call-update) | async-done | bytes 6291472 | tf_op jit(solution)/shard_map/all_gather | solution.py:625
  29.1 4.7 %fusion.49 = f32[256,3072]{1,0:T(8,128)S(1)} fusion(bf16[1024,3072]{1,0:T(8,128)(2,1)} %all-gather.5.cloned.1.call-done, bf16[1,256,1024]{2,1,0:T(8,128)(2,1)S(1)} %copy-done.6), kind=kOutput, calls=%fused_computation.106 | convolution fusion | flops 1610612736 | bytes 9961472 | tf_op jit(solution)/shard_map/td,de->te/dot_general | solution.py:22
  37.3 1.2 copy.35
  38.5 6.8 %all-to-all-start = ((bf16[16,192,256]{2,1,0:T(8,128)(2,1)}), bf16[16,192,256]{2,1,0:T(8,128)(2,1)S(1)}, u32[]{:S(2)}, u32[]{:S(2)}) async-start(bf16[16,192,256]{2,1,0:T(8,128)(2,1)} %bitcast.181), calls=%async_computation | async-start | bytes 3145728 | tf_op jit(solution)/shard_map/all_to_all | solution.py:584
  45.9 33.7 %all-to-all-done.qkv_ref = bf16[16,192,256]{2,1,0:T(8,128)(2,1)S(1)} async-done(((bf16[16,192,256]{2,1,0:T(8,128)(2,1)}), bf16[16,192,256]{2,1,0:T(8,128)(2,1)S(1)}, u32[]{:S(2)}, u32[]{:S(2)}) %all-to-all-start) | async-done | bytes 1572896 | tf_op jit(solution)/shard_map/all_to_all | solution.py:584
  80.7 26.4 %attend_forward.1 = (bf16[16,64,256]{2,1,0:T(8,128)(2,1)}, f32[64,4096]{1,0:T(8,128)}, f32[1,4096]{1,0:T(1,128)}) custom-call(bf16[16,192,256]{2,1,0:T(8,128)(2,1)} %copy-done.1), custom_call_target="tpu_custom_call" | custom-call | tf_op jit(solution)/shard_map/attend_forward/pallas_call | solution.py:392
  107.1 8.4 %all-to-all-start.1 = ((bf16[16,64,256]{2,1,0:T(8,128)(2,1)}), bf16[16,64,256]{2,1,0:T(8,128)(2,1)S(1)}, u32[]{:S(2)}, u32[]{:S(2)}) async-start(bf16[16,64,256]{2,1,0:T(8,128)(2,1)} %get-tuple-element.12), calls=%async_computation.1 | async-start | bytes 1048576 | tf_op jit(solution)/shard_map/all_to_all | solution.py:584
  115.6 14.5 %all-to-all-done.1 = bf16[16,64,256]{2,1,0:T(8,128)(2,1)S(1)} async-done(((bf16[16,64,256]{2,1,0:T(8,128)(2,1)}), bf16[16,64,256]{2,1,0:T(8,128)(2,1)S(1)}, u32[]{:S(2)}, u32[]{:S(2)}) %all-to-all-start.1) | async-done | bytes 524320 | tf_op jit(solution)/shard_map/all_to_all | solution.py:584
  131.0 2.3 convolution_add_fusion.7
  135.4 5.7 %convolution_add_fusion.2 = f32[256,4096]{1,0:T(8,128)S(1)} fusion(bf16[256,1024]{1,0:T(8,128)(2,1)S(1)} %fusion.45, bf16[1024,4096]{1,0:T(8,128)(2,1)} %all-gather.9.cloned.1.call-done, f32[4096]{0:T(1024)S(1)} %copy-done.38), kind=kOutput, calls=%fused_computation.5 | convolution fusion | flops 2148532224 | bytes 13123584 | tf_op jit(solution)/shard_map/td,df->tf/dot_general | solution.py:22
  141.1 12.2 %multiply_convert_fusion = (bf16[256,4096]{1,0:T(8,128)(2,1)S(1)}, f32[256,4096]{1,0:T(8,128)}, f32[256,4096]{1,0:T(8,128)}) fusion(f32[256,4096]{1,0:T(8,128)S(1)} %convolution_add_fusion.2, bf16[256,16]{0,1:T(8,128)(2,1)S(1)} %convolution_convert_fusion.15, bf16[8,16,4096]{2,1,0:T(8,128)(2,1)} %param.30, s32[]{:T(128)S(6)} %select_n.45), kind=kOutput, calls=%fused_computation.17 | convolution fusion | flops 102760448 | bytes 14819332 | tf_op jit(solution)/shard_map/tr,rf->tf/dot_general | solution.py:22
  153.4 1.3 copy-done.4
  154.7 1.5 convolution_convert_fusion.11
  156.3 6.5 %convolution_add_fusion.8 = f32[256,1024]{1,0:T(8,128)S(1)} fusion(bf16[256,4096]{1,0:T(8,128)(2,1)} %copy-done.4, bf16[4096,1024]{1,0:T(8,128)(2,1)} %all-gather.11.cloned.1.call-done, f32[1024]{0:T(1024)S(1)} %bitcast.209), kind=kOutput, calls=%fused_computation.56 | convolution fusion | flops 2147745792 | bytes 11538432 | tf_op jit(solution)/shard_map/tf,fd->td/dot_general | solution.py:22
  163.7 1.3 fusion.86
  165.4 4.4 %fusion.98 = f32[256,4096]{1,0:T(8,128)} fusion(bf16[256,1024]{1,0:T(8,128)(2,1)S(1)} %add_convert_fusion.2, bf16[4096,1024]{1,0:T(8,128)(2,1)S(1)} %bitcast.213), kind=kOutput, calls=%fused_computation.184 | convolution fusion | flops 2147483648 | bytes 13107200 | tf_op jit(solution)/shard_map/td,fd->tf/dot_general | solution.py:22
  169.9 5.9 %fusion.6 = bf16[256,4096]{1,0:T(8,128)(2,1)S(1)} fusion(f32[256,4096]{1,0:T(8,128)} %get-tuple-element.24, f32[256,4096]{1,0:T(8,128)} %fusion.98, bf16[256,16]{0,1:T(8,128)(2,1)S(1)} %convolution_convert_fusion.14, f32[256,4096]{1,0:T(8,128)} %get-tuple-element.59, bf16[8,16,4096]{2,1,0:T(8,128)(2,1)} %param.31, s32[]{:T(128)S(6)} %select_n.45), kind=kOutput, calls=%fused_computation.14 | convolution fusion | flops 51380224 | bytes 14819332 | tf_op jit(solution)/shard_map/tr,rf->tf/dot_general | solution.py:22
  175.7 1.7 convolution_convert_fusion.10
  177.5 2.4 fusion.99
  179.9 1.5 multiply_reduce_fusion
  185.9 18.4 %all_to_all.25.grad_ref = bf16[16,64,256]{2,1,0:T(8,128)(2,1)} all-to-all(bf16[16,64,256]{2,1,0:T(8,128)(2,1)} %bitcast.190), channel_id=1, replica_groups=mesh['ctx'=16,'fsdp'=2] {'ctx'}, dimensions={0} | all-to-all | bytes 1048576 | tf_op jit(solution)/shard_map/all_to_all | solution.py:584
  204.3 51.7 %attend_backward.1 = (bf16[16,64,256]{2,1,0:T(8,128)(2,1)}, bf16[16,256,128]{2,1,0:T(8,128)(2,1)}) custom-call(bf16[16,192,256]{2,1,0:T(8,128)(2,1)} %copy-done.1, bf16[16,64,256]{2,1,0:T(8,128)(2,1)} %all_to_all.25.grad_ref, f32[64,4096]{1,0:T(8,128)} %get-tuple-element.13.context_ref, f32[1,4096]{1,0:T(1,128)} %get-tuple-element.14.lse_ref), custom_call_target="tpu_custom_call" | custom-call | tf_op jit(solution)/shard_map/attend_backward/pallas_call | solution.py:488
  256.0 17.8 %all_to_all.26 = bf16[16,64,256]{2,1,0:T(8,128)(2,1)} all-to-all(bf16[16,64,256]{2,1,0:T(8,128)(2,1)} %get-tuple-element.15), channel_id=1, replica_groups=mesh['ctx'=16,'fsdp'=2] {'ctx'}, dimensions={0} | all-to-all | bytes 1048576 | tf_op jit(solution)/shard_map/all_to_all | solution.py:584
  273.8 4.5 %all-to-all-start.4 = ((bf16[16,256,128]{2,1,0:T(8,128)(2,1)}), bf16[16,256,128]{2,1,0:T(8,128)(2,1)}, u32[]{:S(2)}, u32[]{:S(2)}) async-start(bf16[16,256,128]{2,1,0:T(8,128)(2,1)} %get-tuple-element.16), calls=%async_computation.4 | async-start | bytes 2097152 | tf_op jit(solution)/shard_map/all_to_all | solution.py:584
  279.6 1.8 all-reduce
  282.0 2.0 convolution_convert_fusion
  286.3 2.0 convolution_convert_fusion.1
  290.6 1.5 fusion.32
  292.4 8.5 %all-to-all-done.4 = bf16[16,256,128]{2,1,0:T(8,128)(2,1)} async-done(((bf16[16,256,128]{2,1,0:T(8,128)(2,1)}), bf16[16,256,128]{2,1,0:T(8,128)(2,1)}, u32[]{:S(2)}, u32[]{:S(2)}) %all-to-all-start.4) | async-done | bytes 1048608 | tf_op jit(solution)/shard_map/all_to_all | solution.py:584
  300.9 2.3 copy.38
  303.2 1.3 fusion.88
  306.5 1.6 convolution_convert_fusion.2
  308.1 2.4 convolution_convert_fusion.8
  315.0 36.5 %reduce_terms.1 = bf16[2,16,144,128]{3,2,1,0:T(8,128)(2,1)} custom-call(bf16[16,144,128]{2,1,0:T(8,128)(2,1)} %bitcast.195), custom_call_target="tpu_custom_call" | custom-call | tf_op jit(solution)/shard_map/reduce_terms/pallas_call | solution.py:568
  353.7 1.5 slice_convert_fusion.4
  356.2 1.7 broadcast_in_dim.237
  357.9 1.7 broadcast_in_dim.241
  359.6 1.7 broadcast_in_dim.243
  361.3 1.7 broadcast_in_dim.245
  366.0 1.5 fusion.93
  367.5 1.5 broadcast_in_dim.223
  369.0 1.5 broadcast_in_dim.227
  374.6 5.2 %fusion.24 = f32[256,1024]{1,0:T(8,128)S(1)} fusion(bf16[1024,3072]{1,0:T(8,128)(2,1)} %all-gather.5.cloned.1.call-done, bf16[256,1024]{1,0:T(8,128)(2,1)S(1)} %copy.40, bf16[256,1024]{1,0:T(8,128)(2,1)} %copy.39, bf16[256,1024]{1,0:T(8,128)(2,1)} %bitcast.198, f32[256,1024]{1,0:T(8,128)} %copy-done.10, f32[256]{0:T(256)S(1)} %copy-done.37), kind=kOutput, calls=%fused_computation.55 | convolution fusion | flops 1615855616 | bytes 9962496 | tf_op jit(solution)/shard_map/te,de->td/dot_general | solution.py:22
  379.8 2.3 fusion.23
  382.1 1.9 select_add_fusion
  384.9 1.7 select_add_fusion.3
  386.6 2.7 select_add_fusion.1
  (167 shorter events, 42.3 us)
Async XLA Ops:
  7.2 4.7 %copy-start = (bf16[8,5,16,1024]{3,2,1,0:T(8,128)(2,1)S(1)}, bf16[8,5,16,1024]{3,2,1,0:T(8,128)(2,1)}, u32[]{:S(2)}) copy-start(bf16[8,5,16,1024]{3,2,1,0:T(8,128)(2,1)} %param.29) | copy-start | bytes 3932164
  7.2 2.9 copy-start.33
  7.2 2.9 copy-start.6
  7.2 21.9 %all-gather.5.cloned.1.call-start = ((), (), s32[]{:S(2)}) async-start(), calls=%async_computation.5 | async-start | bytes 9437184 | tf_op jit(solution)/shard_map/all_gather | solution.py:625
  7.9 123.1 %all-gather.7.cloned.1.call-start = ((), (), s32[]{:S(2)}) async-start(), calls=%async_computation.6 | async-start | bytes 3145728 | tf_op jit(solution)/shard_map/all_gather | solution.py:625
  8.7 126.7 %all-gather.9.cloned.1.call-start = ((), (), s32[]{:S(2)}) async-start(), calls=%async_computation.7 | async-start | bytes 12582912 | tf_op jit(solution)/shard_map/all_gather | solution.py:625
  14.1 19.7 %copy-start.35 = (f32[1024]{0:T(1024)S(1)}, f32[1024]{0:T(1024)}, u32[]{:S(2)}) copy-start(f32[1024]{0:T(1024)} %param.24) | copy-start | bytes 12292
  29.1 4.7 %copy-start.2 = (f32[3,256,1024]{2,1,0:T(8,128)S(1)}, f32[3,256,1024]{2,1,0:T(8,128)}, u32[]{:S(2)}) copy-start(f32[3,256,1024]{2,1,0:T(8,128)} %fusion.59) | copy-start | bytes 9437188
  38.5 41.0 %all-to-all-start = ((bf16[16,192,256]{2,1,0:T(8,128)(2,1)}), bf16[16,192,256]{2,1,0:T(8,128)(2,1)S(1)}, u32[]{:S(2)}, u32[]{:S(2)}) async-start(bf16[16,192,256]{2,1,0:T(8,128)(2,1)} %bitcast.181), calls=%async_computation | async-start | bytes 3145728 | tf_op jit(solution)/shard_map/all_to_all | solution.py:584
  45.3 70.3 %copy-start.34 = (f32[2,1024]{1,0:T(2,128)S(1)}, f32[2,1024]{1,0:T(2,128)}, u32[]{:S(2)}) copy-start(f32[2,1024]{1,0:T(2,128)} %param.26) | copy-start | bytes 24580
  45.3 110.9 %all-gather.11.cloned.1.call-start = ((), (), s32[]{:S(2)}) async-start(), calls=%async_computation.8 | async-start | bytes 12582912 | tf_op jit(solution)/shard_map/all_gather | solution.py:625
  79.6 1.1 copy-start.1
  107.1 23.0 %all-to-all-start.1 = ((bf16[16,64,256]{2,1,0:T(8,128)(2,1)}), bf16[16,64,256]{2,1,0:T(8,128)(2,1)S(1)}, u32[]{:S(2)}, u32[]{:S(2)}) async-start(bf16[16,64,256]{2,1,0:T(8,128)(2,1)} %get-tuple-element.12), calls=%async_computation.1 | async-start | bytes 1048576 | tf_op jit(solution)/shard_map/all_to_all | solution.py:584
  131.0 4.3 %copy-start.38 = (f32[4096]{0:T(1024)S(1)}, f32[4096]{0:T(1024)}, u32[]{:S(2)}) copy-start(f32[4096]{0:T(1024)} %param.25) | copy-start | bytes 49156
  135.3 5.8 %copy-start.29 = (bf16[256,16]{0,1:T(8,128)(2,1)}, bf16[256,16]{0,1:T(8,128)(2,1)S(1)}, u32[]{:S(2)}) copy-start(bf16[256,16]{0,1:T(8,128)(2,1)S(1)} %convolution_convert_fusion.15) | copy-start | bytes 24580
  153.4 1.3 copy-start.4
  156.2 9.1 %slice-start.2 = ((s8[8388608]{0:T(1024)(128)(4,1)}), s8[4194304]{0:T(1024)(128)(4,1)S(1)}, s32[]{:S(2)}) async-start(s8[8388608]{0:T(1024)(128)(4,1)} %bitcast.212), calls=%async_computation.11 | async-start | bytes 8388608
  156.2 7.1 %copy-start.12 = (bf16[1,256,1024]{2,1,0:T(8,128)(2,1)S(1)}, bf16[1,256,1024]{2,1,0:T(8,128)(2,1)}, u32[]{:S(2)}) copy-start(bf16[1,256,1024]{2,1,0:T(8,128)(2,1)} %param.17) | copy-start | bytes 1572868
  156.3 9.1 %slice-start.3 = ((s8[8388608]{0:T(1024)(128)(4,1)}), s8[4194304]{0:T(1024)(128)(4,1)S(1)}, s32[]{:S(2)}) async-start(s8[8388608]{0:T(1024)(128)(4,1)} %bitcast.212), calls=%async_computation.12 | async-start | bytes 8388608
  165.0 12.5 %slice-start = ((s8[8388608]{0:T(1024)(128)(4,1)}), s8[4194304]{0:T(1024)(128)(4,1)S(1)}, s32[]{:S(2)}) async-start(s8[8388608]{0:T(1024)(128)(4,1)} %bitcast.210), calls=%async_computation.9 | async-start | bytes 8388608
  165.1 4.7 %copy-start.8 = (bf16[256,1024]{1,0:T(8,128)(2,1)}, bf16[256,1024]{1,0:T(8,128)(2,1)S(1)}, u32[]{:S(2)}) copy-start(bf16[256,1024]{1,0:T(8,128)(2,1)S(1)} %add_convert_fusion.2) | copy-start | bytes 1572868
  165.4 4.5 %copy-start.30 = (bf16[256,16]{0,1:T(8,128)(2,1)}, bf16[256,16]{0,1:T(8,128)(2,1)S(1)}, u32[]{:S(2)}) copy-start(bf16[256,16]{0,1:T(8,128)(2,1)S(1)} %convolution_convert_fusion.14) | copy-start | bytes 24580
  165.4 12.1 %slice-start.1 = ((s8[8388608]{0:T(1024)(128)(4,1)}), s8[4194304]{0:T(1024)(128)(4,1)S(1)}, s32[]{:S(2)}) async-start(s8[8388608]{0:T(1024)(128)(4,1)} %bitcast.210), calls=%async_computation.10 | async-start | bytes 8388608
  175.7 4.1 %copy-start.5 = (bf16[256,4096]{1,0:T(8,128)(2,1)}, bf16[256,4096]{1,0:T(8,128)(2,1)S(1)}, u32[]{:S(2)}) copy-start(bf16[256,4096]{1,0:T(8,128)(2,1)S(1)} %fusion.6) | copy-start | bytes 6291460
  177.5 2.4 copy-start.27
  179.9 3.1 copy-start.3
  181.8 1.0 copy-start.10
  183.0 73.0 %copy-start.28 = (bf16[256,16]{0,1:T(8,128)(2,1)}, bf16[256,16]{0,1:T(8,128)(2,1)S(1)}, u32[]{:S(2)}) copy-start(bf16[256,16]{0,1:T(8,128)(2,1)S(1)} %convolution_convert_fusion.13) | copy-start | bytes 24580
  184.9 93.4 %copy-start.39 = (u32[32]{0:T(128)S(1)}, u32[32]{0:T(128)}, u32[]{:S(2)}) copy-start(u32[32]{0:T(128)} %constant.106) | copy-start | bytes 388
  273.8 16.1 %copy-start.9 = (bf16[256,1024]{1,0:T(8,128)(2,1)S(1)}, bf16[256,1024]{1,0:T(8,128)(2,1)}, u32[]{:S(2)}) copy-start(bf16[256,1024]{1,0:T(8,128)(2,1)} %copy-done.8) | copy-start | bytes 1572868
  273.8 27.1 %all-to-all-start.4 = ((bf16[16,256,128]{2,1,0:T(8,128)(2,1)}), bf16[16,256,128]{2,1,0:T(8,128)(2,1)}, u32[]{:S(2)}, u32[]{:S(2)}) async-start(bf16[16,256,128]{2,1,0:T(8,128)(2,1)} %get-tuple-element.16), calls=%async_computation.4 | async-start | bytes 2097152 | tf_op jit(solution)/shard_map/all_to_all | solution.py:584
  285.7 6.5 %copy-start.11 = (bf16[16,64,256]{2,1,0:T(8,128)(2,1)S(1)}, bf16[16,64,256]{2,1,0:T(8,128)(2,1)}, u32[]{:S(2)}) copy-start(bf16[16,64,256]{2,1,0:T(8,128)(2,1)} %all_to_all.26) | copy-start | bytes 1572868
  292.1 14.3 %copy-start.25 = (bf16[3,16,256]{2,1,0:T(8,128)(2,1)S(1)}, bf16[3,16,256]{2,1,0:T(8,128)(2,1)}, u32[]{:S(2)}) copy-start(bf16[3,16,256]{2,1,0:T(8,128)(2,1)} %copy-done.24) | copy-start | bytes 73732
  292.4 15.7 %copy-start.18 = (bf16[1024,256]{0,1:T(8,128)(2,1)}, bf16[1024,256]{0,1:T(8,128)(2,1)S(1)}, u32[]{:S(2)}) copy-start(bf16[1024,256]{0,1:T(8,128)(2,1)S(1)} %copy.37) | copy-start | bytes 1572868
  306.5 4.0 %copy-start.22 = (bf16[1,16,1024]{2,1,0:T(8,128)(2,1)S(1)}, bf16[1,16,1024]{2,1,0:T(8,128)(2,1)}, u32[]{:S(2)}) copy-start(bf16[1,16,1024]{2,1,0:T(8,128)(2,1)} %fusion.33) | copy-start | bytes 98308
  306.5 4.0 %copy-start.23 = (bf16[1,16,1024]{2,1,0:T(8,128)(2,1)S(1)}, bf16[1,16,1024]{2,1,0:T(8,128)(2,1)}, u32[]{:S(2)}) copy-start(bf16[1,16,1024]{2,1,0:T(8,128)(2,1)} %fusion.34) | copy-start | bytes 98308
  306.5 4.1 %copy-start.7 = (bf16[1,256,1024]{2,1,0:T(8,128)(2,1)S(1)}, bf16[1,256,1024]{2,1,0:T(8,128)(2,1)}, u32[]{:S(2)}) copy-start(bf16[1,256,1024]{2,1,0:T(8,128)(2,1)} %param.16) | copy-start | bytes 1572868
  308.1 6.0 %copy-start.19 = (bf16[512,128]{1,0:T(8,128)(2,1)S(1)}, bf16[512,128]{1,0:T(8,128)(2,1)}, u32[]{:S(2)}) copy-start(bf16[512,128]{1,0:T(8,128)(2,1)} %reshape.176) | copy-start | bytes 393220
  359.6 14.9 %copy-start.37 = (f32[256]{0:T(256)S(1)}, f32[256]{0:T(256)}, u32[]{:S(2)}) copy-start(f32[256]{0:T(256)} %copy-done.36) | copy-start | bytes 3076
  374.5 5.2 %copy-start.26 = (bf16[3,256,16]{1,2,0:T(8,128)(2,1)S(1)}, bf16[3,256,16]{1,2,0:T(8,128)(2,1)}, u32[]{:S(2)}) copy-start(bf16[3,256,16]{1,2,0:T(8,128)(2,1)} %convolution_convert_fusion.8) | copy-start | bytes 73732
  374.5 7.5 %copy-start.31 = (pred[8]{0:T(512)(128)(4,1)S(1)}, pred[8]{0:T(512)(128)(4,1)}, u32[]{:S(2)}) copy-start(pred[8]{0:T(512)(128)(4,1)} %get-tuple-element.55) | copy-start | bytes 28
  374.5 7.5 %copy-start.32 = (pred[8]{0:T(512)(128)(4,1)S(1)}, pred[8]{0:T(512)(128)(4,1)}, u32[]{:S(2)}) copy-start(pred[8]{0:T(512)(128)(4,1)} %get-tuple-element.56) | copy-start | bytes 28
  379.7 4.3 %copy-start.20 = (f32[16,1024]{1,0:T(8,128)S(1)}, f32[16,1024]{1,0:T(8,128)}, u32[]{:S(2)}) copy-start(f32[16,1024]{1,0:T(8,128)} %broadcast_in_dim.223) | copy-start | bytes 196612
  379.7 4.3 %copy-start.21 = (f32[16,1024]{1,0:T(8,128)S(1)}, f32[16,1024]{1,0:T(8,128)}, u32[]{:S(2)}) copy-start(f32[16,1024]{1,0:T(8,128)} %broadcast_in_dim.227) | copy-start | bytes 196612
  379.8 6.9 %copy-start.13 = (f32[16,4096]{1,0:T(8,128)S(1)}, f32[16,4096]{1,0:T(8,128)}, u32[]{:S(2)}) copy-start(f32[16,4096]{1,0:T(8,128)} %broadcast_in_dim.237) | copy-start | bytes 786436
  379.8 6.9 %copy-start.14 = (f32[16,4096]{1,0:T(8,128)S(1)}, f32[16,4096]{1,0:T(8,128)}, u32[]{:S(2)}) copy-start(f32[16,4096]{1,0:T(8,128)} %broadcast_in_dim.241) | copy-start | bytes 786436
  379.8 6.9 %copy-start.15 = (f32[16,4096]{1,0:T(8,128)S(1)}, f32[16,4096]{1,0:T(8,128)}, u32[]{:S(2)}) copy-start(f32[16,4096]{1,0:T(8,128)} %broadcast_in_dim.243) | copy-start | bytes 786436
  379.8 6.8 %copy-start.16 = (f32[16,4096]{1,0:T(8,128)S(1)}, f32[16,4096]{1,0:T(8,128)}, u32[]{:S(2)}) copy-start(f32[16,4096]{1,0:T(8,128)} %broadcast_in_dim.245) | copy-start | bytes 786436
  (3 other events, 2.0 us)
Sparse Core Ops, SparseCore 0:
  9.6 19.4 all-gather.4
  30.6 11.7 all-gather.6
  43.9 21.0 all-gather.8
  66.4 21.0 all-gather.10

commit v3 on v0

--- a/solution.py
+++ b/solution.py
@@ -1,6 +1,10 @@
+import functools
+
 import jax
 import jax.numpy as jnp
 from jax import lax
+from jax.experimental import pallas as pl
+from jax.experimental.pallas import tpu as pltpu
 from jax.sharding import PartitionSpec as P
 
 H = 16
@@ -100,7 +104,7 @@
     return (context, log_total)
 
 
-def body(
+def gather_body(
     tokens,
     cotangent,
     sequence_adapter_index,
@@ -307,9 +311,831 @@
     )
 
 
+BF16 = jnp.bfloat16
+F32 = jnp.float32
+LOG2E = 1.4426950408889634
+VMEM_LIMIT = 60 * 2**20
+MESH = pl.DeviceIdType.MESH
+
+
+def dot32(left, right):
+    return jnp.dot(left, right, preferred_element_type=F32)
+
+
+def dot_nt(left, right):
+    return lax.dot_general(left, right, (((1,), (1,)), ((), ())), preferred_element_type=F32)
+
+
+def dot_tn(left, right):
+    return lax.dot_general(left, right, (((0,), (0,)), ((), ())), preferred_element_type=F32)
+
+
+def split_three(value):
+    high = value.astype(BF16)
+    rest = value - high.astype(F32)
+    middle = rest.astype(BF16)
+    return high, middle, (rest - middle.astype(F32)).astype(BF16)
+
+
+def flip(value):
+    return value.astype(F32).T.astype(BF16)
+
+
+def remote(src, dst, send_sem, recv_sem, ctx, core):
+    return pltpu.make_async_remote_copy(
+        src_ref=src,
+        dst_ref=dst,
+        send_sem=send_sem,
+        recv_sem=recv_sem,
+        device_id=(ctx, core),
+        device_id_type=MESH,
+    )
+
+
+def greet(me, core, peers):
+    barrier = pltpu.get_barrier_semaphore()
+    for step in range(1, peers):
+        pl.semaphore_signal(barrier, inc=1, device_id=(me ^ step, core), device_id_type=MESH)
+    pl.semaphore_signal(barrier, inc=1, device_id=(me, 1 - core), device_id_type=MESH)
+    pl.semaphore_wait(barrier, peers)
+
+
+def forward_kernel(
+    block_q,
+    block_k,
+    x_ref,
+    wqkv_ref,
+    wout_ref,
+    wfc1_ref,
+    wfc2_ref,
+    down_ref,
+    up_ref,
+    biases_ref,
+    value_bias_ref,
+    qkv_ref,
+    arrived_ref,
+    context_ref,
+    lse_ref,
+    rank_ref,
+    wqkv_far,
+    wout_far,
+    wfc1_far,
+    wfc2_far,
+    weight,
+    y,
+    outgoing,
+    leaving,
+    qta,
+    kk,
+    vta,
+    scores,
+    weight_sem,
+    far_sem,
+    near_sem,
+    kv_sem,
+    q_sem,
+    back_sem,
+):
+    peers, _, rows = qkv_ref.shape
+    length = peers * rows
+    width = x_ref.shape[1]
+    depth = width // 2
+    me = lax.axis_index("ctx")
+    core = lax.axis_index("fsdp")
+    other = 1 - core
+    load = pltpu.make_async_copy(wqkv_ref, weight.at[core], weight_sem.at[0])
+    load.start()
+    greet(me, core, peers)
+    fetch = remote(wqkv_ref, weight.at[core], weight_sem.at[1], weight_sem.at[2], me, other)
+    fetch.start()
+
+    halves = ((wout_ref, wout_far), (wfc1_ref, wfc1_far), (wfc2_ref, wfc2_far))
+    far = [
+        remote(half, there, far_sem.at[0, i], far_sem.at[1, i], me, other)
+        for i, (half, there) in enumerate(halves)
+    ]
+
+    rank_low = dot_nt(x_ref[...], down_ref[0:48]).astype(BF16)
+    rank_ref[...] = rank_low
+    x_own = x_ref[:, pl.ds(pl.multiple_of(core * depth, depth), depth)]
+    x_other = x_ref[:, pl.ds(pl.multiple_of(other * depth, depth), depth)]
+    load.wait()
+    for part in (1, 2, 0):
+        cols = slice(part * width, (part + 1) * width)
+        y[:, cols] = dot32(x_own, weight[core, :, cols]) + dot32(rank_low[:, part * 16 : part * 16 + 16], up_ref[part * 16 : part * 16 + 16])
+    fetch.wait_recv()
+
+    def project(part):
+        cols = slice(part * width, (part + 1) * width)
+        value = y[:, cols] + dot32(x_other, weight[other, :, cols])
+        if part == 0:
+            value = (value + biases_ref[0:1, :]) * 0.125
+        if part == 2:
+            value = value + value_bias_ref[...]
+        for two in range(peers // 2):
+            turned = value[:, two * 128 : two * 128 + 128].T.astype(BF16)
+            outgoing[2 * two, part * 64 : part * 64 + 64] = turned[0:64]
+            outgoing[2 * two + 1, part * 64 : part * 64 + 64] = turned[64:128]
+
+    def kv_copy(step):
+        return remote(
+            outgoing.at[me ^ step, 64:192], qkv_ref.at[step, 64:192], kv_sem.at[0, step], kv_sem.at[1, step], me ^ step, core
+        )
+
+    def q_copy(step):
+        return remote(
+            outgoing.at[me ^ step, 0:64], qkv_ref.at[step, 0:64], q_sem.at[0, step], q_sem.at[1, step], me ^ step, core
+        )
+
+    def back_copy(step):
+        return remote(
+            leaving.at[step], arrived_ref.at[me], back_sem.at[0, step], back_sem.at[1, step], me ^ step, core
+        )
+
+    project(1)
+    project(2)
+    for step in range(1, peers):
+        kv_copy(step).start()
+    project(0)
+    for step in range(1, peers):
+        q_copy(step).start()
+    for copy in far:
+        copy.start()
+    save = pltpu.make_async_copy(weight.at[other], wqkv_far, near_sem)
+    save.start()
+    qkv_ref[0] = outgoing[me]
+
+    ones = (lax.broadcasted_iota(jnp.int32, (16, rows), 0) == 0).astype(F32).astype(BF16)
+
+    def take_key(step, _):
+        cols = pl.ds(pl.multiple_of(step * rows, rows), rows)
+
+        @pl.when(step > 0)
+        def _():
+            kv_copy(step).wait_recv()
+
+        key = qkv_ref[step, 64:128, :]
+        kk[cols, :] = flip(jnp.concatenate([key, key], 0))
+        vta[0:64, cols] = qkv_ref[step, 128:192, :]
+        vta[64:80, cols] = ones
+        return 0
+
+    lax.fori_loop(0, peers, take_key, 0)
+    steps = length // block_k
+    group = block_q // rows
+
+    def query_step(i, _):
+        def take_query(part, _):
+            step = i * group + part
+            here = pl.ds(pl.multiple_of(part * rows, rows), rows)
+
+            @pl.when(step > 0)
+            def _():
+                q_copy(step).wait_recv()
+
+            query = qkv_ref[step, 0:64, :].astype(F32) * LOG2E
+            high = query.astype(BF16)
+            qta[0:64, here] = high
+            qta[64:128, here] = (query - high.astype(F32)).astype(BF16)
+            return 0
+
+        lax.fori_loop(0, group, take_query, 0)
+        cols = pl.ds(pl.multiple_of(i * block_q, block_q), block_q)
+        scores[0] = dot32(kk[pl.ds(0, block_k), :], qta[...])
+
+        def half(j, now, carry):
+            running, total = carry
+            later = jnp.minimum(j + 1, steps - 1)
+            here = pl.ds(pl.multiple_of(j * block_k, block_k), block_k)
+            there = pl.ds(pl.multiple_of(later * block_k, block_k), block_k)
+            scores[1 - now] = dot32(kk[there, :], qta[...])
+            block = scores[now]
+            new = jnp.maximum(running, jnp.max(block, 0, keepdims=True))
+            weights = jnp.exp2(block - new).astype(BF16)
+            return new, total * jnp.exp2(running - new) + dot32(vta[:, here], weights)
+
+        def pair(j, carry):
+            return half(2 * j + 1, 1, half(2 * j, 0, carry))
+
+        start = (jnp.full((1, block_q), -jnp.inf, F32), jnp.zeros((80, block_q), F32))
+        top, total = lax.fori_loop(0, steps // 2, pair, start)
+        weight_sum = total[64:65]
+        context = total[0:64] / weight_sum
+        context_ref[:, cols] = context
+        lse_ref[:, cols] = top + jnp.log2(weight_sum)
+        low = context.astype(BF16)
+        for part in range(group):
+            step = i * group + part
+            leaving[step] = low[:, part * rows : (part + 1) * rows]
+
+            @pl.when(step > 0)
+            def _():
+                back_copy(step).start()
+
+        return 0
+
+    lax.fori_loop(0, length // block_q, query_step, 0)
+    arrived_ref[me] = leaving[0]
+    for step in range(1, peers):
+        back_copy(step).wait_recv()
+    for step in range(1, peers):
+        kv_copy(step).wait_send()
+        q_copy(step).wait_send()
+        back_copy(step).wait_send()
+    fetch.wait_send()
+    for copy in far:
+        copy.wait()
+    save.wait()
+
+
+def attend_forward(x, wqkv, wout, wfc1, wfc2, down, up, biases, value_bias):
+    rows, width = x.shape
+    peers = H
+    length = peers * rows
+    block_q, block_k = 1024, 512
+    vmem = pl.BlockSpec(memory_space=pltpu.VMEM)
+    hbm = pl.BlockSpec(memory_space=pl.ANY)
+
+    return pl.pallas_call(
+        functools.partial(forward_kernel, block_q, block_k),
+        out_shape=[
+            jax.ShapeDtypeStruct((peers, 192, rows), BF16),
+            jax.ShapeDtypeStruct((peers, 64, rows), BF16),
+            jax.ShapeDtypeStruct((64, length), F32),
+            jax.ShapeDtypeStruct((1, length), F32),
+            jax.ShapeDtypeStruct((rows, 48), BF16),
+            *(jax.ShapeDtypeStruct(half.shape, BF16) for half in (wqkv, wout, wfc1, wfc2)),
+        ],
+        in_specs=[vmem] + [hbm] * 4 + [vmem] * 4,
+        out_specs=[vmem] * 5 + [hbm] * 4,
+        scratch_shapes=[
+            pltpu.VMEM((2,) + wqkv.shape, BF16),
+            pltpu.VMEM((rows, 3 * width), F32),
+            pltpu.VMEM((peers, 192, rows), BF16),
+            pltpu.VMEM((peers, 64, rows), BF16),
+            pltpu.VMEM((128, block_q), BF16),
+            pltpu.VMEM((length, 128), BF16),
+            pltpu.VMEM((80, length), BF16),
+            pltpu.VMEM((2, block_k, block_q), F32),
+            pltpu.SemaphoreType.DMA((3,)),
+            pltpu.SemaphoreType.DMA((2, 3)),
+            pltpu.SemaphoreType.DMA,
+            pltpu.SemaphoreType.DMA((2, peers)),
+            pltpu.SemaphoreType.DMA((2, peers)),
+            pltpu.SemaphoreType.DMA((2, peers)),
+        ],
+        compiler_params=pltpu.CompilerParams(
+            collective_id=1, has_side_effects=True, vmem_limit_bytes=VMEM_LIMIT
+        ),
+        name="attend_forward",
+    )(x, wqkv, wout, wfc1, wfc2, down, up, biases, value_bias)
+
+
+def sum_copies(mine, parts, total, sems, me, core):
+    peers = mine.shape[0]
+    scatter = [
+        remote(mine.at[me ^ step], parts.at[step], sems.at[0, step], sems.at[1, step], me ^ step, core)
+        for step in range(1, peers)
+    ]
+    gather = [
+        remote(total.at[core, me], total.at[core, me], sems.at[2, step], sems.at[3, step], me ^ step, core)
+        for step in range(1, peers)
+    ]
+    last = remote(total.at[core], total.at[core], sems.at[0, 0], sems.at[1, 0], me, 1 - core)
+    return scatter, gather, last
+
+
+def sum_parts(scatter, mine, parts, total, me, core):
+    value = mine[me].astype(F32)
+    for step, copy in enumerate(scatter, 1):
+        copy.wait_recv()
+        value = value + parts[step].astype(F32)
+    total[core, me] = value.astype(BF16)
+
+
+def put_term(mine, base, term):
+    units = mine.shape[2] // 128
+    for unit in range(term.shape[1] // 128):
+        at = base // 128 + unit
+        lanes = slice(at % units * 128, at % units * 128 + 128)
+        mine[at // units, :, lanes] = term[:, unit * 128 : unit * 128 + 128].astype(BF16)
+
+
+def backward_kernel(
+    block_q,
+    block_k,
+    x_ref,
+    cotangent_ref,
+    qkv_ref,
+    arrived_ref,
+    context_ref,
+    lse_ref,
+    rank_ref,
+    wqkv_ref,
+    wqkv_far,
+    wout_ref,
+    wout_far,
+    wfc1_ref,
+    wfc1_far,
+    wfc2_ref,
+    wfc2_far,
+    down_ref,
+    out_down_ref,
+    up_ref,
+    hidden_up_ref,
+    hidden_down_ref,
+    biases_ref,
+    hidden_bias_ref,
+    gains_ref,
+    outcome_ref,
+    grad_ref,
+    mlp_ref,
+    att_ref,
+    wout,
+    wfc1,
+    wfc2,
+    slope,
+    act,
+    grad_resid,
+    mlp_mine,
+    mlp_parts,
+    att_mine,
+    att_parts,
+    outgoing,
+    incoming,
+    qta,
+    gta,
+    kk,
+    vv,
+    kt,
+    both,
+    dqt,
+    dq_out,
+    dq_in,
+    dkv_out,
+    dkv_in,
+    joined,
+    load_sem,
+    grad_sem,
+    dq_sem,
+    dkv_sem,
+    mlp_sem,
+    att_sem,
+):
+    peers, _, rows = qkv_ref.shape
+    length = peers * rows
+    width = x_ref.shape[1]
+    hidden = hidden_bias_ref.shape[1]
+    me = lax.axis_index("ctx")
+    core = lax.axis_index("fsdp")
+    wqkv = wfc1.at[:, 0 : 3 * width]
+
+    loads = []
+    for i, (half, far, full) in enumerate(
+        (
+            (wout_ref, wout_far, wout),
+            (wfc1_ref, wfc1_far, wfc1),
+            (wfc2_ref, wfc2_far, wfc2),
+            (wqkv_ref, wqkv_far, wqkv),
+        )
+    ):
+        count = half.shape[0]
+        for j, (source, owner) in enumerate(((half, core), (far, 1 - core))):
+            place = full.at[pl.ds(pl.multiple_of(owner * count, count), count), :]
+            loads.append(pltpu.make_async_copy(source, place, load_sem.at[i, j]))
+    for copy in loads[:6]:
+        copy.start()
+    greet(me, core, peers)
+
+    def mean(value):
+        return jnp.mean(value, -1, keepdims=True)
+
+    def norm_backward(grad, hat, scale):
+        return scale * (grad - mean(grad) - hat * mean(grad * hat))
+
+    def up(j):
+        return up_ref[16 * j : 16 * j + 16]
+
+    def down(j):
+        return down_ref[16 * j : 16 * j + 16]
+
+    context_low = flip(arrived_ref[...].reshape(width, rows))
+    rank_out = dot_nt(context_low, out_down_ref[...]).astype(BF16)
+    loads[0].wait()
+    loads[1].wait()
+    resid = x_ref[...].astype(F32) + dot32(context_low, wout[...]) + biases_ref[1:2] + dot32(rank_out, up(3))
+    center = resid - mean(resid)
+    scale_one = lax.rsqrt(mean(center * center) + EPSILON)
+    hat_one = center * scale_one
+    normed = hat_one * gains_ref[0:1] + biases_ref[3:4]
+    normed_low = normed.astype(BF16)
+    rank_one = dot_nt(normed_low, down(3)).astype(BF16)
+    loads[2].wait()
+    loads[3].wait()
+    loads[4].wait()
+    loads[5].wait()
+    piece = 1024
+    rank_two = jnp.zeros((rows, 16), F32)
+    mixed = normed + biases_ref[2:3]
+    for part in range(hidden // piece):
+        cols = slice(part * piece, (part + 1) * piece)
+        pre = (
+            dot32(normed_low, wfc1[:, cols])
+            + hidden_bias_ref[:, cols]
+            + dot32(rank_one, hidden_up_ref[:, cols])
+        )
+        share = 0.5 + 0.5 * lax.erf(pre * 0.7071067811865476)
+        slope[:, cols] = share + pre * (0.3989422804014327 * jnp.exp(-0.5 * pre * pre))
+        active = (pre * share).astype(BF16)
+        act[:, cols] = active
+        rank_two = rank_two + dot_nt(active, hidden_down_ref[:, cols])
+        mixed = mixed + dot32(active, wfc2[cols, :])
+    rank_two = rank_two.astype(BF16)
+    mixed = mixed + dot32(rank_two, up(4))
+    center = mixed - mean(mixed)
+    scale_two = lax.rsqrt(mean(center * center) + EPSILON)
+    hat_two = center * scale_two
+    outcome_ref[...] = (hat_two * gains_ref[1:2] + biases_ref[4:5]).astype(BF16)
+    grad_sum = norm_backward(cotangent_ref[...].astype(F32) * gains_ref[1:2], hat_two, scale_two)
+    grad_mixed = grad_sum.astype(BF16)
+    put_term(mlp_mine, 2 * hidden, dot_tn(rank_two, grad_mixed))
+    grad_rank = dot_nt(grad_mixed, up(4)).astype(BF16)
+    put_term(mlp_mine, 0, dot_tn(grad_rank, act[...]))
+    grad_one = jnp.zeros((rows, 16), F32)
+    grad_normed = jnp.zeros((rows, width), F32)
+    for part in range(hidden // piece):
+        cols = slice(part * piece, (part + 1) * piece)
+        grad_act = dot_nt(grad_mixed, wfc2[cols, :]) + dot32(grad_rank, hidden_down_ref[:, cols])
+        grad_hidden = (grad_act.astype(BF16).astype(F32) * slope[:, cols]).astype(BF16)
+        put_term(mlp_mine, hidden + part * piece, dot_tn(rank_one, grad_hidden))
+        grad_one = grad_one + dot_nt(grad_hidden, hidden_up_ref[:, cols])
+        grad_normed = grad_normed + dot_nt(grad_hidden, wfc1[:, cols])
+    grad_one = grad_one.astype(BF16)
+    put_term(mlp_mine, 2 * hidden + width, dot_tn(grad_one, normed_low))
+    grad_normed = (grad_normed + dot32(grad_one, down(3))).astype(BF16).astype(F32)
+    resid_grad = norm_backward((grad_sum + grad_normed) * gains_ref[0:1], hat_one, scale_one)
+    grad_resid[...] = resid_grad
+    grad_branch = resid_grad.astype(BF16)
+    put_term(mlp_mine, 2 * hidden + 2 * width, dot_tn(rank_out, grad_branch))
+    grad_rank = dot_nt(grad_branch, up(3)).astype(BF16)
+    put_term(mlp_mine, 2 * hidden + 3 * width, dot_tn(grad_rank, context_low))
+    turned = dot_nt(wout[...], grad_branch) + lax.dot_general(
+        out_down_ref[...], grad_rank, (((0,), (1,)), ((), ())), preferred_element_type=F32
+    )
+    outgoing[...] = turned.astype(BF16).reshape(peers, 64, rows)
+
+    loads[6].start()
+    loads[7].start()
+
+    def grad_copy(step):
+        return remote(
+            outgoing.at[me ^ step], incoming.at[step], grad_sem.at[0, step], grad_sem.at[1, step], me ^ step, core
+        )
+
+    for step in range(1, peers):
+        grad_copy(step).start()
+    mlp_scatter, mlp_gather, mlp_last = sum_copies(mlp_mine, mlp_parts, mlp_ref, mlp_sem, me, core)
+    for copy in mlp_scatter:
+        copy.start()
+    incoming[0] = outgoing[me]
+
+    row_at = lax.broadcasted_iota(jnp.int32, (16, rows), 0)
+    minus = jnp.where(lax.broadcasted_iota(jnp.int32, (rows, 16), 1) < 3, -1.0, 0.0).astype(BF16)
+    minus_rows = jnp.where(lax.broadcasted_iota(jnp.int32, (64, rows), 0) < 3, -1.0, 0.0).astype(BF16)
+
+    def tail(value):
+        high, middle, low = (part.astype(F32) for part in split_three(value))
+        return jnp.where(row_at == 0, high, jnp.where(row_at == 1, middle, jnp.where(row_at == 2, low, 0.0))).astype(
+            BF16
+        )
+
+    def prepare(step, _):
+        cols = pl.ds(pl.multiple_of(step * rows, rows), rows)
+        query = qkv_ref[step, 0:64, :].astype(F32) * LOG2E
+        high = query.astype(BF16)
+        qta[0:64, cols] = high
+        qta[64:128, cols] = (query - high.astype(F32)).astype(BF16)
+        qta[128:144, cols] = tail(lse_ref[:, cols])
+        key = qkv_ref[step, 64:128, :]
+        kt[:, cols] = key
+        kk[cols, 0:128] = flip(jnp.concatenate([key, key], 0))
+        kk[cols, 128:144] = minus
+        vv[cols, :] = flip(jnp.concatenate([qkv_ref[step, 128:192, :], minus_rows], 0))
+        gta[80:128, cols] = jnp.zeros((48, rows), BF16)
+        return 0
+
+    lax.fori_loop(0, peers, prepare, 0)
+
+    def take_grad(step, _):
+        cols = pl.ds(pl.multiple_of(step * rows, rows), rows)
+
+        @pl.when(step > 0)
+        def _():
+            grad_copy(step).wait_recv()
+
+        grad = incoming[step]
+        gta[0:64, cols] = grad
+        gta[64:80, cols] = tail(jnp.sum(grad.astype(F32) * context_ref[:, cols], 0, keepdims=True))
+        both[cols, :] = flip(jnp.concatenate([qkv_ref[step, 0:64, :], grad], 0))
+        return 0
+
+    lax.fori_loop(0, peers, take_grad, 0)
+    dqt[...] = jnp.zeros_like(dqt)
+    first = lax.broadcasted_iota(jnp.int32, (block_k, 128), 1) < 64
+    key_steps = length // block_k
+    query_group = block_q // rows
+    key_group = block_k // rows
+
+    def dq_copy(step):
+        return remote(dq_out.at[step], dq_in.at[me], dq_sem.at[0, step], dq_sem.at[1, step], me ^ step, core)
+
+    def dkv_copy(step):
+        return remote(dkv_out.at[step], dkv_in.at[me], dkv_sem.at[0, step], dkv_sem.at[1, step], me ^ step, core)
+
+    def key_step(i, last):
+        here = pl.ds(pl.multiple_of(i * block_k, block_k), block_k)
+
+        def query_step(j, carry):
+            dk, dv = carry
+            cols = pl.ds(pl.multiple_of(j * block_q, block_q), block_q)
+            probs = jnp.exp2(dot32(kk[here, :], qta[:, cols]))
+            change = dot32(vv[here, :], gta[:, cols])
+            low = (probs * change).astype(BF16)
+            dv = dv + dot32(probs.astype(BF16), both[cols, :])
+            dk = dk + dot32(low, both[cols, :])
+            dq = dqt[:, cols] + dot32(kt[:, here], low)
+            if not last:
+                dqt[:, cols] = dq
+            else:
+                done = dq.astype(BF16)
+                for part in range(query_group):
+                    step = j * query_group + part
+                    dq_out[step] = done[:, part * rows : (part + 1) * rows]
+
+                    @pl.when(step > 0)
+                    def _():
+                        dq_copy(step).start()
+
+            return dk, dv
+
+        start = jnp.zeros((block_k, 128), F32)
+        dk, dv = lax.fori_loop(0, length // block_q, query_step, (start, start))
+        dkv = jnp.where(first, dk, dv).astype(BF16)
+        for part in range(key_group):
+            step = i * key_group + part
+            dkv_out[step] = dkv[part * rows : (part + 1) * rows]
+
+            @pl.when(step > 0)
+            def _():
+                dkv_copy(step).start()
+
+    def key_steps_of(low, high):
+        def one(i, _):
+            key_step(i, False)
+            return 0
+
+        lax.fori_loop(low, high, one, 0)
+
+    third = (key_steps - 1) // 3
+    key_steps_of(0, third)
+    sum_parts(mlp_scatter, mlp_mine, mlp_parts, mlp_ref, me, core)
+    for copy in mlp_gather:
+        copy.start()
+    key_steps_of(third, 2 * third)
+    for copy in mlp_gather:
+        copy.wait_recv()
+    mlp_last.start()
+    key_steps_of(2 * third, key_steps - 1)
+    key_step(key_steps - 1, True)
+
+    dq_in[me] = dq_out[0]
+    dkv_in[me] = dkv_out[0]
+    for step in range(1, peers):
+        dq_copy(step).wait_recv()
+        dkv_copy(step).wait_recv()
+    joined[:, 0:width] = (dq_in[...].reshape(width, rows).astype(F32).T * 0.125).astype(BF16)
+    left = lax.broadcasted_iota(jnp.int32, (rows, 128), 1) < 64
+    for two in range(peers // 2):
+        even = dkv_in[2 * two].astype(F32)
+        odd = dkv_in[2 * two + 1].astype(F32)
+        cols = slice(width + two * 128, width + two * 128 + 128)
+        joined[:, cols] = jnp.where(left, even, pltpu.roll(odd, 64, 1)).astype(BF16)
+        cols = slice(2 * width + two * 128, 2 * width + two * 128 + 128)
+        joined[:, cols] = jnp.where(left, pltpu.roll(even, 64, 1), odd).astype(BF16)
+    ranks = []
+    for part in range(3):
+        grad = joined[:, part * width : (part + 1) * width]
+        rank = dot_nt(grad, up(part)).astype(BF16)
+        ranks.append(rank)
+        put_term(att_mine, part * width, dot_tn(rank_ref[:, part * 16 : part * 16 + 16], grad))
+        put_term(att_mine, (3 + part) * width, dot_tn(rank, x_ref[...]))
+    att_scatter, att_gather, att_last = sum_copies(att_mine, att_parts, att_ref, att_sem, me, core)
+    for copy in att_scatter:
+        copy.start()
+    loads[6].wait()
+    loads[7].wait()
+    total = grad_resid[...] + dot_nt(joined[...], wqkv[...])
+    for part in range(3):
+        total = total + dot32(ranks[part], down(part))
+    grad_ref[...] = total
+    sum_parts(att_scatter, att_mine, att_parts, att_ref, me, core)
+    for copy in att_gather:
+        copy.start()
+    for copy in att_gather:
+        copy.wait_recv()
+    att_last.start()
+    for step in range(1, peers):
+        grad_copy(step).wait_send()
+        dq_copy(step).wait_send()
+        dkv_copy(step).wait_send()
+    for copy in mlp_scatter + mlp_gather + att_scatter + att_gather:
+        copy.wait_send()
+    mlp_last.wait()
+    att_last.wait()
+
+
+def run_backward(
+    x,
+    cotangent,
+    saved,
+    weights,
+    down,
+    out_down,
+    up,
+    hidden_up,
+    hidden_down,
+    biases,
+    hidden_bias,
+    gains,
+):
+    rows, width = x.shape
+    peers = H
+    length = peers * rows
+    hidden = hidden_bias.shape[1]
+    block_q, block_k = 1024, 512
+    vmem = pl.BlockSpec(memory_space=pltpu.VMEM)
+    hbm = pl.BlockSpec(memory_space=pl.ANY)
+    mlp_part = (2 * hidden + 4 * width) // peers
+    att_part = 6 * width // peers
+    return pl.pallas_call(
+        functools.partial(backward_kernel, block_q, block_k),
+        out_shape=[
+            jax.ShapeDtypeStruct((rows, width), BF16),
+            jax.ShapeDtypeStruct((rows, width), F32),
+            jax.ShapeDtypeStruct((2, peers, 16, mlp_part), BF16),
+            jax.ShapeDtypeStruct((2, peers, 16, att_part), BF16),
+        ],
+        in_specs=[vmem] * 7 + [hbm] * 8 + [vmem] * 8,
+        out_specs=[vmem] * 4,
+        scratch_shapes=[
+            pltpu.VMEM((width, width), BF16),
+            pltpu.VMEM((width, hidden), BF16),
+            pltpu.VMEM((hidden, width), BF16),
+            pltpu.VMEM((rows, hidden), F32),
+            pltpu.VMEM((rows, hidden), BF16),
+            pltpu.VMEM((rows, width), F32),
+            pltpu.VMEM((peers, 16, mlp_part), BF16),
+            pltpu.VMEM((peers, 16, mlp_part), BF16),
+            pltpu.VMEM((peers, 16, att_part), BF16),
+            pltpu.VMEM((peers, 16, att_part), BF16),
+            pltpu.VMEM((peers, 64, rows), BF16),
+            pltpu.VMEM((peers, 64, rows), BF16),
+            pltpu.VMEM((144, length), BF16),
+            pltpu.VMEM((128, length), BF16),
+            pltpu.VMEM((length, 144), BF16),
+            pltpu.VMEM((length, 128), BF16),
+            pltpu.VMEM((64, length), BF16),
+            pltpu.VMEM((length, 128), BF16),
+            pltpu.VMEM((64, length), F32),
+            pltpu.VMEM((peers, 64, rows), BF16),
+            pltpu.VMEM((peers, 64, rows), BF16),
+            pltpu.VMEM((peers, rows, 128), BF16),
+            pltpu.VMEM((peers, rows, 128), BF16),
+            pltpu.VMEM((rows, 3 * width), BF16),
+            pltpu.SemaphoreType.DMA((4, 2)),
+            pltpu.SemaphoreType.DMA((2, peers)),
+            pltpu.SemaphoreType.DMA((2, peers)),
+            pltpu.SemaphoreType.DMA((2, peers)),
+            pltpu.SemaphoreType.DMA((4, peers)),
+            pltpu.SemaphoreType.DMA((4, peers)),
+        ],
+        compiler_params=pltpu.CompilerParams(
+            collective_id=2, has_side_effects=True, vmem_limit_bytes=VMEM_LIMIT
+        ),
+        name="run_backward",
+    )(x, cotangent, *saved, *weights, down, out_down, up, hidden_up, hidden_down, biases, hidden_bias, gains)
+
+
+def heads_body(
+    tokens,
+    cotangent,
+    sequence_adapter_index,
+    query_key_value_weight,
+    output_weight,
+    first_feed_weight,
+    second_feed_weight,
+    biases,
+    value_bias_vector,
+    first_feed_bias,
+    norm_gain_pair,
+    adapter_down_factors,
+    output_down_factor,
+    adapter_up_factors,
+    hidden_up_factor,
+    hidden_down_factor,
+):
+    _, rows, width = tokens.shape
+    adapter_number = adapter_down_factors.shape[0]
+    tokens = tokens[0]
+    cotangent = cotangent[0]
+
+    def pick(table):
+        return lax.dynamic_index_in_dim(table, sequence_adapter_index[0], 0, keepdims=False)
+
+    down, out_down, up, hidden_up, hidden_down = (
+        pick(table)
+        for table in (
+            adapter_down_factors,
+            output_down_factor,
+            adapter_up_factors,
+            hidden_up_factor,
+            hidden_down_factor,
+        )
+    )
+
+    down = down.reshape(-1, width)
+    up = up.reshape(-1, width)
+    *saved, wqkv_far, wout_far, wfc1_far, wfc2_far = attend_forward(
+        tokens,
+        query_key_value_weight,
+        output_weight,
+        first_feed_weight,
+        second_feed_weight,
+        down,
+        up,
+        biases,
+        value_bias_vector[None],
+    )
+    weights = (
+        query_key_value_weight,
+        wqkv_far,
+        output_weight,
+        wout_far,
+        first_feed_weight,
+        wfc1_far,
+        second_feed_weight,
+        wfc2_far,
+    )
+    outcome, grad_tokens, mlp_terms, att_terms = run_backward(
+        tokens,
+        cotangent,
+        saved,
+        weights,
+        down,
+        out_down,
+        up,
+        hidden_up,
+        hidden_down,
+        biases,
+        first_feed_bias[None],
+        norm_gain_pair,
+    )
+
+    def side_by_side(terms):
+        return terms.astype(F32).transpose(0, 2, 1, 3).reshape(2, 16, -1)
+
+    mlp_terms = side_by_side(mlp_terms)
+    att_terms = side_by_side(att_terms)
+    hidden = first_feed_bias.shape[0]
+    term_hd = mlp_terms[:, :, :hidden]
+    term_uh = mlp_terms[:, :, hidden : 2 * hidden]
+    term_u2, term_d1, term_uo, term_do = (
+        mlp_terms[:, :, 2 * hidden + i * width : 2 * hidden + (i + 1) * width] for i in range(4)
+    )
+    term_at = [att_terms[:, :, i * width : (i + 1) * width] for i in range(6)]
+    totals = (
+        jnp.stack([*term_at[3:], term_d1], 1),
+        term_do,
+        jnp.stack([*term_at[:3], term_uo, term_u2], 1),
+        term_uh,
+        term_hd,
+    )
+    index_all = lax.all_gather(sequence_adapter_index, "fsdp", axis=0, tiled=True)
+    picker = index_all[:, None] == jnp.arange(adapter_number, dtype=jnp.int32)[None, :]
+    tables = []
+    for every in totals:
+        table = 0.0
+        for seq in range(2):
+            mask = picker[seq].reshape((adapter_number,) + (1,) * (every.ndim - 1))
+            table = table + jnp.where(mask, every[seq][None], 0.0)
+        tables.append(table)
+    return (outcome[None], grad_tokens[None], *tables)
+
+
 def solution(mesh):
+    one_head_each = mesh.shape["ctx"] == H and mesh.shape["fsdp"] == 2
     return jax.shard_map(
-        body,
+        heads_body if one_head_each else gather_body,
         mesh=mesh,
         in_specs=(
             P("fsdp", "ctx", None),

time: 1090 us -> 225 us (0.21)
  waiting for transfers between devices: 697 us -> 0 us
  matrix products: 247 us -> 0 us
  Pallas kernels: 0 us -> 201 us
  local copies, waits for them, and re-layouts: 81.7 us -> 10.3 us
  other arithmetic: 30.3 us -> 9.76 us
  between operations: 15.8 us -> 1.55 us
  loops' own time: 11.6 us -> 0 us
    reduce_scatter x2 -> x0, waiting for transfers between devices: 330 us -> none  [the longest x1 183 us: body(): lax.psum_scatter(grad_key_all.reshape(seq_count, length, model_width).ast...]
    dot_general x93 -> x0, matrix products: 247 us -> none  [the longest x76 204 us: plain_sum(): return jnp.einsum(form, left, right, preferred_element_type=jnp.float32)]
    pallas_call x0 -> x2, Pallas kernels: none -> 201 us  [the longest x1 130 us: run_backward(): pl.pallas_call(functools.partial(backward_kernel, block_q, block_k), out_...]
    psum x1 -> x0, waiting for transfers between devices: 189 us -> none  [body(): lax.psum((mlp_hup, mlp_hdown, mlp_fc1, mlp_fc2), ('ctx', 'fsdp'))]
    all_gather x6 -> x0, waiting for transfers between devices: 175 us -> none  [the longest x1 100 us: body(): lax.all_gather(keys_own, 'ctx', axis=1, tiled=True)]
    convert_element_type x4 -> x0, local copies, waits for them, and re-layouts: 25.4 us -> none  [the longest x1 12 us: body(): grad_key_all.reshape(seq_count, length, model_width).astype(jnp.bfloat16)]
    all_gather x2 -> x0, local copies, waits for them, and re-layouts: 23.9 us -> none  [the longest x1 12.1 us: body(): lax.all_gather(values_own, 'ctx', axis=1, tiled=True)]
    reduce_sum x13 -> x0, other arithmetic: 12.5 us -> none  [the longest x8 8.93 us: max_step(): jnp.sum(jnp.exp(scores - new_max[..., None]), -1)]
  transfers between devices with their start and end apart: 9 -> 0, of which waited for: 6 -> 0; matrix products, arithmetic and copies ran while one was open for 17% -> 0% of each run, Pallas kernels for 0% -> 0%
where the time goes in v3:
time: 225 us
  Pallas kernels  201 us (89%)
  local copies, waits for them, and re-layouts  10.3 us (5%)
  other arithmetic  9.76 us (4%)
    pallas_call x1, Pallas kernels, run_backward(): pl.pallas_call(functools.partial(backward_kernel, block_q, block_k), out_...  130 us
    pallas_call x1, Pallas kernels, attend_forward(): pl.pallas_call(functools.partial(forward_kernel, block_q, block_k), out_s...  71.3 us
    add x4, other arithmetic, heads_body(): table = table + jnp.where(mask, every[seq][None], 0.0)  8.28 us

profile of v3, /device:TPU:0, one launch (start us, length us, event | category | flops | bytes accessed | tf_op | source)
XLA Modules:
  0.0 224.5 jit_solution(2910019954388403012)
XLA Ops:
  0.6 0.0 copy-start
  1.4 0.6 copy-done
  2.0 0.7 constant_dynamic-slice_fusion
  2.6 1.6 constant_dynamic-slice_fusion.1
  4.2 71.3 %attend_forward.1 = (bf16[16,192,256]{2,1,0:T(8,128)(2,1)}, bf16[16,64,256]{2,1,0:T(8,128)(2,1)}, f32[64,4096]{1,0:T(8,128)}, f32[1,4096]{1,0:T(1,128)}, bf16[25...) custom-call(bf16[256,1024]{1,0:T(8,128)(2,1)} %bitcast.88, ...), custom_call_target="tpu_custom_call" | custom-call | tf_op jit(solution)/shard_map/attend_forward/pallas_call | solution.py:559
  75.5 1.7 dynamic-slice_bitcast_fusion
  77.2 1.4 dynamic-slice_bitcast_fusion.2.out_down_ref
  78.6 129.8 %run_backward.1 = (bf16[256,1024]{1,0:T(8,128)(2,1)}, f32[256,1024]{1,0:T(8,128)}, bf16[2,16,16,768]{3,2,1,0:T(8,128)(2,1)}, bf16[2,16,16,384]{3,2,1,0:T(8,128)(2,1)}) custom-call(bf16[256,1024]{1,0:T(8,128)(2,1)} %bitcast.89, bf16[256,1024]{1,0:T(8,128)(2,1)} %bitcast.95, bf16[16,192,256]{2,1,0:T(8,128)(2,1)} %get-tuple-element.20.qkv_ref, ...), custom_call_target="tpu_custom_call" | custom-call | tf_op jit(solution)/shard_map/run_backward/pallas_call | solution.py:980
  208.4 1.3 convert_bitcast_fusion
  209.7 0.0 copy-start.4
  209.7 0.1 copy.26
  209.9 0.9 slice_bitcast_fusion.3
  210.8 0.0 copy-done.4
  210.8 0.6 dynamic-slice
  211.3 0.8 dynamic-update-slice
  212.1 1.8 all-reduce
  213.9 0.1 iota_compare_fusion
  214.0 0.0 copy-start.3
  214.0 3.7 %select_add_fusion.1 = (f32[8,16,4096]{2,1,0:T(8,128)}, f32[8,16,4096]{2,1,0:T(8,128)}) fusion(f32[16,4096]{1,0:T(8,128)S(1)} %get-tuple-element.34, f32[16,4096]{1,0:T(8,128)S(1)} %get-tuple-element.33, pred[8]{0:T(512)(128)(4,1)S(1)} %get-tuple-element.49, pred[8]{0:T(512)(128)(4,1)S(1)} %get-tuple-element.48, f32[16,4096]{1,0:T(8,128)} %get-tuple-element.35, ...), kind=kLoop, calls=%fused_computation.1 | loop fusion | flops 3145728 | bytes 5242896 | tf_op jit(solution)/shard_map/add | solution.py:1130
  217.8 0.0 copy-done.3
  217.8 0.1 convert_bitcast_fusion.1
  217.8 0.1 copy.25
  218.0 1.9 select_add_fusion
  220.0 0.9 select_add_fusion.4
  221.0 0.0 copy-start.2
  221.1 0.0 copy-start.1
  221.1 1.7 select_add_fusion.3
  222.8 0.0 copy-done.2
  222.8 0.8 copy.35
  223.6 0.0 copy-done.1
  223.6 1.0 copy.36
  (13 shorter events, 0.2 us)
Async XLA Ops:
  0.6 1.3 copy-start
  209.7 1.0 copy-start.4
  214.0 3.7 %copy-start.3 = (bf16[2,16,16,384]{3,2,1,0:T(8,128)(2,1)S(1)}, bf16[2,16,16,384]{3,2,1,0:T(8,128)(2,1)}, u32[]{:S(2)}) copy-start(bf16[2,16,16,384]{3,2,1,0:T(8,128)(2,1)} %get-tuple-element.31) | copy-start | bytes 1179652
  221.0 1.8 copy-start.2
  221.1 2.5 %copy-start.1 = (f32[256,1024]{1,0:T(8,128)S(1)}, f32[256,1024]{1,0:T(8,128)}, u32[]{:S(2)}) copy-start(f32[256,1024]{1,0:T(8,128)} %get-tuple-element.30) | copy-start | bytes 3145732

commit v4 on v0

--- a/solution.py
+++ b/solution.py
@@ -1,6 +1,10 @@
+import functools
+
 import jax
 import jax.numpy as jnp
 from jax import lax
+from jax.experimental import pallas as pl
+from jax.experimental.pallas import tpu as pltpu
 from jax.sharding import PartitionSpec as P
 
 H = 16
@@ -100,7 +104,7 @@
     return (context, log_total)
 
 
-def body(
+def gather_body(
     tokens,
     cotangent,
     sequence_adapter_index,
@@ -307,9 +311,920 @@
     )
 
 
+BF16 = jnp.bfloat16
+F32 = jnp.float32
+LOG2E = 1.4426950408889634
+VMEM_LIMIT = 60 * 2**20
+MESH = pl.DeviceIdType.MESH
+
+
+def dot32(left, right):
+    return jnp.dot(left, right, preferred_element_type=F32)
+
+
+def dot_nt(left, right):
+    return lax.dot_general(left, right, (((1,), (1,)), ((), ())), preferred_element_type=F32)
+
+
+def dot_tn(left, right):
+    return lax.dot_general(left, right, (((0,), (0,)), ((), ())), preferred_element_type=F32)
+
+
+def split_three(value):
+    high = value.astype(BF16)
+    rest = value - high.astype(F32)
+    middle = rest.astype(BF16)
+    return high, middle, (rest - middle.astype(F32)).astype(BF16)
+
+
+def flip(value):
+    return value.astype(F32).T.astype(BF16)
+
+
+def remote(src, dst, send_sem, recv_sem, device):
+    return pltpu.make_async_remote_copy(
+        src_ref=src,
+        dst_ref=dst,
+        send_sem=send_sem,
+        recv_sem=recv_sem,
+        device_id=device,
+        device_id_type=MESH,
+    )
+
+
+class Place:
+    def __init__(self):
+        self.ctx = lax.axis_index("ctx")
+        self.core = lax.axis_index("fsdp")
+        self.half = self.ctx // (H // 2)
+        self.low = self.ctx % (H // 2)
+        self.me = self.low * 2 + self.core
+        self.swaps = self.core != self.half
+        self.pair = (self.core + self.half) % 2
+        self.sibling = (self.ctx, 1 - self.core)
+        self.partner = ((self.ctx + H // 2) % H, 1 - self.core)
+
+    def peer(self, step):
+        number = self.me ^ step
+        return (self.half * (H // 2) + number // 2, number % 2)
+
+    def greet(self):
+        barrier = pltpu.get_barrier_semaphore()
+        for step in range(1, H):
+            pl.semaphore_signal(barrier, inc=1, device_id=self.peer(step), device_id_type=MESH)
+        pl.semaphore_signal(barrier, inc=1, device_id=self.partner, device_id_type=MESH)
+        pl.semaphore_wait(barrier, H)
+
+
+def sum_copies(mine, parts, total, sems, place):
+    own = total.at[place.low, place.pair, place.half]
+    both = total.at[place.low, place.pair]
+    scatter = [
+        remote(mine.at[place.me ^ step], parts.at[step], sems.at[0, step], sems.at[1, step], place.peer(step))
+        for step in range(1, H)
+    ]
+    cross = remote(own, own, sems.at[0, 0], sems.at[1, 0], place.partner)
+    gather = [
+        remote(both, both, sems.at[2, step], sems.at[3, step], place.peer(step))
+        for step in range(1, H)
+    ]
+    return scatter, cross, gather
+
+
+def sum_parts(scatter, mine, parts, total, place):
+    value = mine[place.me].astype(F32)
+    for step, copy in enumerate(scatter, 1):
+        copy.wait_recv()
+        value = value + parts[step].astype(F32)
+    total[place.low, place.pair, place.half] = value.astype(BF16)
+
+
+def put_term(mine, base, term):
+    units = mine.shape[2] // 128
+    for unit in range(term.shape[1] // 128):
+        at = base // 128 + unit
+        lanes = slice(at % units * 128, at % units * 128 + 128)
+        mine[at // units, :, lanes] = term[:, unit * 128 : unit * 128 + 128].astype(BF16)
+
+
+def layer_kernel(
+    block_q,
+    block_k,
+    index_ref,
+    tokens_ref,
+    cotangent_ref,
+    wqkv_ref,
+    wout_ref,
+    wfc1_ref,
+    wfc2_ref,
+    down_table,
+    up_table,
+    out_down_table,
+    hidden_up_table,
+    hidden_down_table,
+    biases_ref,
+    value_bias_ref,
+    hidden_bias_ref,
+    gains_ref,
+    outcome_ref,
+    grad_ref,
+    index_out,
+    hidden_down_out,
+    hidden_up_out,
+    down_out,
+    up_out,
+    out_down_out,
+    wqkv_far,
+    wfc1_far,
+    wide,
+    wfc2,
+    wout,
+    big,
+    act,
+    small,
+    small_hidden,
+    x,
+    cotangent,
+    rank_att,
+    outgoing,
+    qkv,
+    leaving,
+    arrived,
+    incoming,
+    context,
+    qta,
+    gta,
+    kk,
+    vv,
+    kt,
+    both,
+    dqt,
+    dq_in,
+    dkv_out,
+    dkv_in,
+    grad_out,
+    grad_in,
+    mlp_mine,
+    mlp_parts,
+    mlp_total,
+    att_mine,
+    att_parts,
+    att_total,
+    load_sem,
+    core_sem,
+    swap_sem,
+    kv_sem,
+    q_sem,
+    back_sem,
+    grad_sem,
+    dq_sem,
+    dkv_sem,
+    mlp_sem,
+    att_sem,
+):
+    peers, _, rows = qkv.shape
+    length = peers * rows
+    width = x.shape[1]
+    depth = width // 2
+    hidden = hidden_bias_ref.shape[1]
+    adapters = hidden_up_table.shape[0] // 16
+    place = Place()
+    me, core = place.me, place.core
+    other = 1 - core
+    wqkv = wide.at[:, 0 : 3 * width]
+    up_at = down_table.shape[0]
+    out_down_at = up_at + up_table.shape[0]
+
+    def half_of(full, owner):
+        count = full.shape[0] // 2
+        return full.at[pl.ds(pl.multiple_of(owner * count, count), count), :]
+
+    def load(source, target, number):
+        return pltpu.make_async_copy(source, target, load_sem.at[number])
+
+    def to_sibling(source, target, number):
+        return remote(source, target, core_sem.at[0, number], core_sem.at[1, number], place.sibling)
+
+    load_wqkv = load(wqkv_ref, half_of(wqkv, core), 0)
+    load_wout = load(wout_ref, half_of(wout, core), 1)
+    load_tables = [
+        load(down_table, wfc2.at[0:up_at], 2),
+        load(up_table, wfc2.at[up_at:out_down_at], 3),
+        load(out_down_table, wfc2.at[out_down_at : out_down_at + out_down_table.shape[0]], 4),
+        load(hidden_up_table, act.at[0 : 16 * adapters], 5),
+        load(hidden_down_table, act.at[16 * adapters : 32 * adapters], 6),
+    ]
+    load_x = load(tokens_ref, x, 7)
+    load_cotangent = load(cotangent_ref, cotangent, 8)
+    load_wfc1 = load(wfc1_ref, half_of(wide, core), 9)
+    load_wfc1_far = load(wfc1_far, half_of(wide, other), 10)
+    load_wfc2 = load(wfc2_ref, half_of(wfc2, core), 11)
+    again_wqkv = load(wqkv_ref, half_of(wqkv, core), 12)
+    again_wqkv_far = load(wqkv_far, half_of(wqkv, other), 13)
+    give_wqkv = to_sibling(wqkv_ref, half_of(wqkv, core), 0)
+    give_wout = to_sibling(wout_ref, half_of(wout, core), 1)
+    give_index = to_sibling(index_out.at[core], index_out.at[core], 2)
+    count = small.shape[0]
+    give_small = [to_sibling(small, wide.at[0:count, 3 * width : 4 * width], 3)] + [
+        to_sibling(
+            small_hidden.at[:, part * width : (part + 1) * width],
+            wide.at[count + 32 * part : count + 32 * part + 32, 3 * width : 4 * width],
+            4 + part,
+        )
+        for part in range(hidden // width)
+    ]
+    give_wfc2 = to_sibling(wfc2_ref, half_of(wfc2, core), 8)
+    give_wfc1 = to_sibling(wfc1_ref, wfc1_far, 9)
+    give_wqkv_again = to_sibling(wqkv_ref, wqkv_far, 10)
+    swap_x = remote(tokens_ref, x, swap_sem.at[0, 0], swap_sem.at[1, 0], place.partner)
+    swap_cotangent = remote(cotangent_ref, cotangent, swap_sem.at[0, 1], swap_sem.at[1, 1], place.partner)
+
+    load_wqkv.start()
+    for copy in load_tables:
+        copy.start()
+    load_wout.start()
+
+    @pl.when(jnp.logical_not(place.swaps))
+    def _():
+        load_x.start()
+        load_cotangent.start()
+
+    adapter = index_ref[0]
+    index_out[core] = jnp.full(index_out.shape[1:], adapter, jnp.int32).astype(F32)
+    place.greet()
+
+    @pl.when(place.swaps)
+    def _():
+        swap_x.start()
+
+    give_wqkv.start()
+    give_index.start()
+
+    for copy in load_tables:
+        copy.wait()
+
+    def select(table, base, group, groups, target, at):
+        chosen = jnp.full((16, table.shape[1]), adapter, jnp.int32)
+        value = jnp.zeros((16, table.shape[1]), F32)
+        for number in range(adapters):
+            start = pl.multiple_of(base + 16 * (number * groups + group), 16)
+            value = jnp.where(chosen == number, table[pl.ds(start, 16), :].astype(F32), value)
+        target[pl.ds(pl.multiple_of(at + 16 * group, 16), 16), :] = value.astype(BF16)
+
+    def select_down(group, _):
+        select(wfc2, 0, group, 4, small, 0)
+        return 0
+
+    def select_up(group, _):
+        select(wfc2, up_at, group, 5, small, 64)
+        return 0
+
+    lax.fori_loop(0, 4, select_down, 0)
+    lax.fori_loop(0, 5, select_up, 0)
+    select(wfc2, out_down_at, 0, 1, small, 144)
+    for part in range(2):
+        select(act, 16 * adapters * part, 0, 1, small_hidden, 16 * part)
+    for copy in give_small:
+        copy.start()
+    give_wout.start()
+    for copy in give_small:
+        copy.wait()
+
+    @pl.when(place.swaps)
+    def _():
+        small[...] = wide[0:count, 3 * width : 4 * width]
+        for part in range(hidden // width):
+            small_hidden[:, part * width : (part + 1) * width] = wide[
+                count + 32 * part : count + 32 * part + 32, 3 * width : 4 * width
+            ]
+
+    hidden_up_ref = small_hidden.at[0:16]
+    hidden_down_ref = small_hidden.at[16:32]
+    out_down_ref = small.at[144:160]
+
+    def down(j):
+        return small[16 * j : 16 * j + 16]
+
+    def up(j):
+        return small[64 + 16 * j : 80 + 16 * j]
+
+    load_wfc2.start()
+    give_wfc2.start()
+
+    @pl.when(place.swaps)
+    def _():
+        swap_x.wait_recv()
+
+    @pl.when(jnp.logical_not(place.swaps))
+    def _():
+        load_x.wait()
+
+    rank_att[...] = dot_nt(x[...], small[0:48]).astype(BF16)
+    x_own = x[:, pl.ds(pl.multiple_of(core * depth, depth), depth)]
+    x_other = x[:, pl.ds(pl.multiple_of(other * depth, depth), depth)]
+    load_wqkv.wait()
+    for part in (1, 2, 0):
+        cols = slice(part * width, (part + 1) * width)
+        big[part * rows : (part + 1) * rows] = dot32(x_own, half_of(wqkv, core)[:, cols]) + dot32(
+            rank_att[:, part * 16 : part * 16 + 16], up(part)
+        )
+    give_wqkv.wait_recv()
+
+    def project(part):
+        cols = slice(part * width, (part + 1) * width)
+        value = big[part * rows : (part + 1) * rows] + dot32(x_other, half_of(wqkv, other)[:, cols])
+        if part == 0:
+            value = (value + biases_ref[0:1, :]) * 0.125
+        if part == 2:
+            value = value + value_bias_ref[...]
+        for two in range(peers // 2):
+            turned = value[:, two * 128 : two * 128 + 128].T.astype(BF16)
+            outgoing[2 * two, part * 64 : part * 64 + 64] = turned[0:64]
+            outgoing[2 * two + 1, part * 64 : part * 64 + 64] = turned[64:128]
+
+    def kv_copy(step):
+        return remote(
+            outgoing.at[me ^ step, 64:192], qkv.at[step, 64:192], kv_sem.at[0, step], kv_sem.at[1, step], place.peer(step)
+        )
+
+    def q_copy(step):
+        return remote(
+            outgoing.at[me ^ step, 0:64], qkv.at[step, 0:64], q_sem.at[0, step], q_sem.at[1, step], place.peer(step)
+        )
+
+    def back_copy(step):
+        return remote(leaving.at[step], arrived.at[me], back_sem.at[0, step], back_sem.at[1, step], place.peer(step))
+
+    project(1)
+    project(2)
+    for step in range(1, peers):
+        kv_copy(step).start()
+    project(0)
+    for step in range(1, peers):
+        q_copy(step).start()
+    give_wfc1.start()
+    give_wqkv_again.start()
+    load_wfc1.start()
+
+    @pl.when(place.swaps)
+    def _():
+        swap_cotangent.start()
+
+    qkv[0] = outgoing[me]
+
+    row_at = lax.broadcasted_iota(jnp.int32, (16, rows), 0)
+    ones = (row_at == 0).astype(F32).astype(BF16)
+    minus = jnp.where(lax.broadcasted_iota(jnp.int32, (rows, 16), 1) < 3, -1.0, 0.0).astype(BF16)
+    minus_rows = jnp.where(lax.broadcasted_iota(jnp.int32, (64, rows), 0) < 3, -1.0, 0.0).astype(BF16)
+
+    def tail(value):
+        at = lax.broadcasted_iota(jnp.int32, (16, value.shape[1]), 0)
+        high, middle, low = (part.astype(F32) for part in split_three(value))
+        return jnp.where(at == 0, high, jnp.where(at == 1, middle, jnp.where(at == 2, low, 0.0))).astype(BF16)
+
+    def take_key(step, _):
+        cols = pl.ds(pl.multiple_of(step * rows, rows), rows)
+
+        @pl.when(step > 0)
+        def _():
+            kv_copy(step).wait_recv()
+
+        key = qkv[step, 64:128, :]
+        value = qkv[step, 128:192, :]
+        kt[:, cols] = key
+        kk[cols, 0:128] = flip(jnp.concatenate([key, key], 0))
+        kk[cols, 128:144] = minus
+        vv[cols, :] = flip(jnp.concatenate([value, minus_rows], 0))
+        gta[0:64, cols] = value
+        gta[64:80, cols] = ones
+        gta[80:128, cols] = jnp.zeros((48, rows), BF16)
+        return 0
+
+    lax.fori_loop(0, peers, take_key, 0)
+    steps = length // block_k
+    group = block_q // rows
+
+    def forward_step(i, _):
+        def take_query(part, _):
+            step = i * group + part
+            here = pl.ds(pl.multiple_of(step * rows, rows), rows)
+
+            @pl.when(step > 0)
+            def _():
+                q_copy(step).wait_recv()
+
+            query = qkv[step, 0:64, :].astype(F32) * LOG2E
+            high = query.astype(BF16)
+            qta[0:64, here] = high
+            qta[64:128, here] = (query - high.astype(F32)).astype(BF16)
+            return 0
+
+        lax.fori_loop(0, group, take_query, 0)
+        cols = pl.ds(pl.multiple_of(i * block_q, block_q), block_q)
+        query = qta.at[0:128, cols]
+        block = dot32(kk[0:block_k, 0:128], query[...])
+        big[0:block_k] = block
+
+        def half(j, now, carry):
+            peak, running, total = carry
+            later = jnp.minimum(j + 1, steps - 1)
+            here = pl.ds(pl.multiple_of(j * block_k, block_k), block_k)
+            there = pl.ds(pl.multiple_of(later * block_k, block_k), block_k)
+            ahead = dot32(kk[there, 0:128], query[...])
+            big[(1 - now) * block_k : (2 - now) * block_k] = ahead
+            new = jnp.maximum(running, peak)
+            weights = jnp.exp2(big[now * block_k : (now + 1) * block_k] - new).astype(BF16)
+            total = total * jnp.exp2(running - new) + dot32(gta[0:80, here], weights)
+            return jnp.max(ahead, 0, keepdims=True), new, total
+
+        def pair(j, carry):
+            return half(2 * j + 1, 1, half(2 * j, 0, carry))
+
+        start = (
+            jnp.max(block, 0, keepdims=True),
+            jnp.full((1, block_q), -jnp.inf, F32),
+            jnp.zeros((80, block_q), F32),
+        )
+        _, top, total = lax.fori_loop(0, steps // 2, pair, start)
+        weight_sum = total[64:65]
+        result = total[0:64] / weight_sum
+        context[:, cols] = result
+        qta[128:144, cols] = tail(top + jnp.log2(weight_sum))
+        low = result.astype(BF16)
+        for part in range(group):
+            step = i * group + part
+            leaving[step] = low[:, part * rows : (part + 1) * rows]
+
+            @pl.when(step > 0)
+            def _():
+                back_copy(step).start()
+
+        return 0
+
+    lax.fori_loop(0, 1, forward_step, 0)
+    give_wfc1.wait_recv()
+    load_wfc1_far.start()
+    lax.fori_loop(1, length // block_q, forward_step, 0)
+    arrived[me] = leaving[0]
+
+    def mean(value):
+        return jnp.mean(value, -1, keepdims=True)
+
+    def norm_backward(grad, hat, scale):
+        return scale * (grad - mean(grad) - hat * mean(grad * hat))
+
+    load_wout.wait()
+    give_wout.wait_recv()
+    for step in range(1, peers):
+        back_copy(step).wait_recv()
+    context_low = flip(arrived[...].reshape(width, rows))
+    rank_out = dot_nt(context_low, out_down_ref[...]).astype(BF16)
+    resid = x[...].astype(F32) + dot32(context_low, wout[...]) + biases_ref[1:2] + dot32(rank_out, up(3))
+    center = resid - mean(resid)
+    scale_one = lax.rsqrt(mean(center * center) + EPSILON)
+    hat_one = center * scale_one
+    normed = hat_one * gains_ref[0:1] + biases_ref[3:4]
+    normed_low = normed.astype(BF16)
+    rank_one = dot_nt(normed_low, down(3)).astype(BF16)
+    load_wfc1.wait()
+    load_wfc1_far.wait()
+    load_wfc2.wait()
+    give_wfc2.wait_recv()
+    piece = 1024
+    rank_two = jnp.zeros((rows, 16), F32)
+    mixed = normed + biases_ref[2:3]
+    for part in range(hidden // piece):
+        cols = slice(part * piece, (part + 1) * piece)
+        pre = (
+            dot32(normed_low, wide[:, cols])
+            + hidden_bias_ref[:, cols]
+            + dot32(rank_one, hidden_up_ref[:, cols])
+        )
+        share = 0.5 + 0.5 * lax.erf(pre * 0.7071067811865476)
+        big[part * rows : (part + 1) * rows] = share + pre * (0.3989422804014327 * jnp.exp(-0.5 * pre * pre))
+        active = (pre * share).astype(BF16)
+        act[:, cols] = active
+        rank_two = rank_two + dot_nt(active, hidden_down_ref[:, cols])
+        mixed = mixed + dot32(active, wfc2[cols, :])
+    rank_two = rank_two.astype(BF16)
+    mixed = mixed + dot32(rank_two, up(4))
+    center = mixed - mean(mixed)
+    scale_two = lax.rsqrt(mean(center * center) + EPSILON)
+    hat_two = center * scale_two
+
+    @pl.when(place.swaps)
+    def _():
+        swap_cotangent.wait_recv()
+
+    @pl.when(jnp.logical_not(place.swaps))
+    def _():
+        load_cotangent.wait()
+
+    grad_sum = norm_backward(cotangent[...].astype(F32) * gains_ref[1:2], hat_two, scale_two)
+    outcome = cotangent
+    outcome[...] = (hat_two * gains_ref[1:2] + biases_ref[4:5]).astype(BF16)
+    home_outcome = remote(outcome, outcome_ref, swap_sem.at[0, 2], swap_sem.at[1, 2], place.partner)
+
+    @pl.when(place.swaps)
+    def _():
+        home_outcome.start()
+
+    @pl.when(jnp.logical_not(place.swaps))
+    def _():
+        outcome_ref[...] = outcome[...]
+
+    grad_mixed = grad_sum.astype(BF16)
+    put_term(mlp_mine, 2 * hidden, dot_tn(rank_two, grad_mixed))
+    grad_rank = dot_nt(grad_mixed, up(4)).astype(BF16)
+    put_term(mlp_mine, 0, dot_tn(grad_rank, act[...]))
+    grad_one = jnp.zeros((rows, 16), F32)
+    grad_normed = jnp.zeros((rows, width), F32)
+    for part in range(hidden // piece):
+        cols = slice(part * piece, (part + 1) * piece)
+        grad_act = dot_nt(grad_mixed, wfc2[cols, :]) + dot32(grad_rank, hidden_down_ref[:, cols])
+        grad_hidden = (grad_act.astype(BF16).astype(F32) * big[part * rows : (part + 1) * rows]).astype(BF16)
+        put_term(mlp_mine, hidden + part * piece, dot_tn(rank_one, grad_hidden))
+        grad_one = grad_one + dot_nt(grad_hidden, hidden_up_ref[:, cols])
+        grad_normed = grad_normed + dot_nt(grad_hidden, wide[:, cols])
+    grad_one = grad_one.astype(BF16)
+    put_term(mlp_mine, 2 * hidden + width, dot_tn(grad_one, normed_low))
+    grad_normed = (grad_normed + dot32(grad_one, down(3))).astype(BF16).astype(F32)
+    resid_grad = norm_backward((grad_sum + grad_normed) * gains_ref[0:1], hat_one, scale_one)
+    grad_resid = big.at[0:rows]
+    grad_resid[...] = resid_grad
+    grad_branch = resid_grad.astype(BF16)
+    put_term(mlp_mine, 2 * hidden + 2 * width, dot_tn(rank_out, grad_branch))
+    grad_rank = dot_nt(grad_branch, up(3)).astype(BF16)
+    put_term(mlp_mine, 2 * hidden + 3 * width, dot_tn(grad_rank, context_low))
+    turned = dot_nt(wout[...], grad_branch) + lax.dot_general(
+        out_down_ref[...], grad_rank, (((0,), (1,)), ((), ())), preferred_element_type=F32
+    )
+    for step in range(1, peers):
+        kv_copy(step).wait_send()
+        q_copy(step).wait_send()
+        back_copy(step).wait_send()
+    outgoing[:, 0:64] = turned.astype(BF16).reshape(peers, 64, rows)
+
+    def grad_copy(step):
+        return remote(
+            outgoing.at[me ^ step, 0:64], incoming.at[step], grad_sem.at[0, step], grad_sem.at[1, step], place.peer(step)
+        )
+
+    for step in range(1, peers):
+        grad_copy(step).start()
+    mlp_scatter, mlp_cross, mlp_gather = sum_copies(mlp_mine, mlp_parts, mlp_total, mlp_sem, place)
+    for copy in mlp_scatter:
+        copy.start()
+    incoming[0] = outgoing[me, 0:64]
+    give_wqkv_again.wait_recv()
+    again_wqkv.start()
+    again_wqkv_far.start()
+    dqt[...] = jnp.zeros_like(dqt)
+
+    def take_grad(step, _):
+        cols = pl.ds(pl.multiple_of(step * rows, rows), rows)
+
+        @pl.when(step > 0)
+        def _():
+            grad_copy(step).wait_recv()
+
+        grad = incoming[step]
+        gta[0:64, cols] = grad
+        gta[64:80, cols] = tail(jnp.sum(grad.astype(F32) * context[:, cols], 0, keepdims=True))
+        both[cols, :] = flip(jnp.concatenate([qkv[step, 0:64, :], grad], 0))
+        return 0
+
+    lax.fori_loop(0, peers, take_grad, 0)
+    first = lax.broadcasted_iota(jnp.int32, (block_k, 128), 1) < 64
+    key_group = block_k // rows
+    dq_out = leaving
+
+    def dq_copy(step):
+        return remote(dq_out.at[step], dq_in.at[me], dq_sem.at[0, step], dq_sem.at[1, step], place.peer(step))
+
+    def dkv_copy(step):
+        return remote(dkv_out.at[step], dkv_in.at[me], dkv_sem.at[0, step], dkv_sem.at[1, step], place.peer(step))
+
+    def key_step(i, last):
+        here = pl.ds(pl.multiple_of(i * block_k, block_k), block_k)
+
+        def query_step(j, carry):
+            dk, dv = carry
+            cols = pl.ds(pl.multiple_of(j * block_q, block_q), block_q)
+            probs = jnp.exp2(dot32(kk[here, :], qta[:, cols]))
+            change = dot32(vv[here, :], gta[:, cols])
+            low = (probs * change).astype(BF16)
+            dv = dv + dot32(probs.astype(BF16), both[cols, :])
+            dk = dk + dot32(low, both[cols, :])
+            dq = dqt[:, cols] + dot32(kt[:, here], low)
+            if not last:
+                dqt[:, cols] = dq
+            else:
+                done = dq.astype(BF16)
+                for part in range(group):
+                    step = j * group + part
+                    dq_out[step] = done[:, part * rows : (part + 1) * rows]
+
+                    @pl.when(step > 0)
+                    def _():
+                        dq_copy(step).start()
+
+            return dk, dv
+
+        start = jnp.zeros((block_k, 128), F32)
+        dk, dv = lax.fori_loop(0, length // block_q, query_step, (start, start))
+        dkv = jnp.where(first, dk, dv).astype(BF16)
+        for part in range(key_group):
+            step = i * key_group + part
+            dkv_out[step] = dkv[part * rows : (part + 1) * rows]
+
+            @pl.when(step > 0)
+            def _():
+                dkv_copy(step).start()
+
+    def key_steps_of(low, high):
+        def one(i, _):
+            key_step(i, False)
+            return 0
+
+        lax.fori_loop(low, high, one, 0)
+
+    third = (steps - 1) // 3
+    key_steps_of(0, third)
+    sum_parts(mlp_scatter, mlp_mine, mlp_parts, mlp_total, place)
+    mlp_cross.start()
+    key_steps_of(third, 2 * third)
+    mlp_cross.wait_recv()
+    for copy in mlp_gather:
+        copy.start()
+    key_steps_of(2 * third, steps - 1)
+    key_step(steps - 1, True)
+
+    for copy in mlp_gather:
+        copy.wait_recv()
+
+    def spread(total, parts):
+        units = total.shape[4] // 128
+        for half in range(2):
+            for unit in range(peers * units):
+                peer = unit // units
+                lanes = slice(unit % units * 128, unit % units * 128 + 128)
+                for target, low, high in parts:
+                    if low <= unit * 128 < high:
+                        at = unit * 128 - low
+                        target(half)[:, at : at + 128] = total[peer // 2, (peer % 2 + half) % 2, half, :, lanes]
+
+    spread(
+        mlp_total,
+        (
+            (lambda half: hidden_down_out.at[half], 0, hidden),
+            (lambda half: hidden_up_out.at[half], hidden, 2 * hidden),
+            (lambda half: up_out.at[half, 4], 2 * hidden, 2 * hidden + width),
+            (lambda half: down_out.at[half, 3], 2 * hidden + width, 2 * hidden + 2 * width),
+            (lambda half: up_out.at[half, 3], 2 * hidden + 2 * width, 2 * hidden + 3 * width),
+            (lambda half: out_down_out.at[half], 2 * hidden + 3 * width, 2 * hidden + 4 * width),
+        ),
+    )
+
+    joined = act.at[:, 0 : 3 * width]
+    dq_in[me] = dq_out[0]
+    dkv_in[me] = dkv_out[0]
+    for step in range(1, peers):
+        dkv_copy(step).wait_recv()
+    left = lax.broadcasted_iota(jnp.int32, (rows, 128), 1) < 64
+    for two in range(peers // 2):
+        even = dkv_in[2 * two].astype(F32)
+        odd = dkv_in[2 * two + 1].astype(F32)
+        cols = slice(width + two * 128, width + two * 128 + 128)
+        joined[:, cols] = jnp.where(left, even, pltpu.roll(odd, 64, 1)).astype(BF16)
+        cols = slice(2 * width + two * 128, 2 * width + two * 128 + 128)
+        joined[:, cols] = jnp.where(left, pltpu.roll(even, 64, 1), odd).astype(BF16)
+    for step in range(1, peers):
+        dq_copy(step).wait_recv()
+    joined[:, 0:width] = (dq_in[...].reshape(width, rows).astype(F32).T * 0.125).astype(BF16)
+    ranks = []
+    for part in range(3):
+        grad = joined[:, part * width : (part + 1) * width]
+        rank = dot_nt(grad, up(part)).astype(BF16)
+        ranks.append(rank)
+        put_term(att_mine, part * width, dot_tn(rank_att[:, part * 16 : part * 16 + 16], grad))
+        put_term(att_mine, (3 + part) * width, dot_tn(rank, x[...]))
+    att_scatter, att_cross, att_gather = sum_copies(att_mine, att_parts, att_total, att_sem, place)
+    for copy in att_scatter:
+        copy.start()
+    again_wqkv.wait()
+    again_wqkv_far.wait()
+    piece = width // 4
+    home = [
+        remote(
+            grad_out.at[:, part * piece : (part + 1) * piece],
+            grad_in.at[:, part * piece : (part + 1) * piece],
+            swap_sem.at[0, 3 + part],
+            swap_sem.at[1, 3 + part],
+            place.partner,
+        )
+        for part in range(4)
+    ]
+    for part in range(4):
+        cols = slice(part * piece, (part + 1) * piece)
+        total = grad_resid[:, cols] + dot_nt(joined[...], wqkv[cols, :])
+        for j in range(3):
+            total = total + dot32(ranks[j], small[16 * j : 16 * j + 16, cols])
+        grad_ref[:, cols] = total
+        grad_out[:, cols] = total.astype(BF16)
+
+        @pl.when(place.swaps)
+        def _():
+            home[part].start()
+
+    sum_parts(att_scatter, att_mine, att_parts, att_total, place)
+    att_cross.start()
+    att_cross.wait_recv()
+    for copy in att_gather:
+        copy.start()
+
+    @pl.when(place.swaps)
+    def _():
+        for part in range(4):
+            home[part].wait_recv()
+            cols = slice(part * piece, (part + 1) * piece)
+            grad_ref[:, cols] = grad_in[:, cols].astype(F32)
+        for part in range(4):
+            home[part].wait_send()
+        home_outcome.wait()
+        swap_x.wait_send()
+        swap_cotangent.wait_send()
+
+    for copy in att_gather:
+        copy.wait_recv()
+    spread(
+        att_total,
+        tuple(
+            (functools.partial(lambda part, half: up_out.at[half, part], part), part * width, (part + 1) * width)
+            for part in range(3)
+        )
+        + tuple(
+            (functools.partial(lambda part, half: down_out.at[half, part], part), (3 + part) * width, (4 + part) * width)
+            for part in range(3)
+        ),
+    )
+    for step in range(1, peers):
+        grad_copy(step).wait_send()
+        dq_copy(step).wait_send()
+        dkv_copy(step).wait_send()
+    for copy in mlp_scatter + mlp_gather + att_scatter + att_gather + [mlp_cross, att_cross]:
+        copy.wait_send()
+    for copy in (give_wqkv, give_wout, give_wfc2, give_wfc1, give_wqkv_again):
+        copy.wait_send()
+    give_index.wait()
+
+
+def run_layer(index, tokens, cotangent, weights, tables, biases, value_bias, hidden_bias, gains):
+    rows, width = tokens.shape
+    peers = H
+    length = peers * rows
+    hidden = hidden_bias.shape[1]
+    block_q, block_k = 1024, 512
+    vmem = pl.BlockSpec(memory_space=pltpu.VMEM)
+    hbm = pl.BlockSpec(memory_space=pl.ANY)
+    mlp_part = (2 * hidden + 4 * width) // peers
+    att_part = 6 * width // peers
+
+    def out(shape, dtype=BF16):
+        return jax.ShapeDtypeStruct(shape, dtype)
+
+    def total(part):
+        return pltpu.VMEM((peers // 2, 2, 2, 16, part), BF16)
+
+    def heads(*shape):
+        return pltpu.VMEM((peers,) + shape, BF16)
+
+    def sems(*shape):
+        return pltpu.SemaphoreType.DMA(shape)
+
+    return pl.pallas_call(
+        functools.partial(layer_kernel, block_q, block_k),
+        out_shape=[
+            out((rows, width)),
+            out((rows, width), F32),
+            out((2, 8, 128), F32),
+            out((2, 16, hidden)),
+            out((2, 16, hidden)),
+            out((2, 4, 16, width)),
+            out((2, 5, 16, width)),
+            out((2, 16, width)),
+            out(weights[0].shape),
+            out(weights[2].shape),
+        ],
+        in_specs=[pl.BlockSpec(memory_space=pltpu.SMEM)] + [hbm] * 11 + [vmem] * 4,
+        out_specs=[vmem] * 8 + [hbm] * 2,
+        scratch_shapes=[
+            pltpu.VMEM((width, hidden), BF16),
+            pltpu.VMEM((hidden, width), BF16),
+            pltpu.VMEM((width, width), BF16),
+            pltpu.VMEM((max(4 * rows, 2 * block_k), 1024), F32),
+            pltpu.VMEM((rows, hidden), BF16),
+            pltpu.VMEM((160, width), BF16),
+            pltpu.VMEM((32, hidden), BF16),
+            pltpu.VMEM((rows, width), BF16),
+            pltpu.VMEM((rows, width), BF16),
+            pltpu.VMEM((rows, 48), BF16),
+            heads(192, rows),
+            heads(192, rows),
+            heads(64, rows),
+            heads(64, rows),
+            heads(64, rows),
+            pltpu.VMEM((64, length), F32),
+            pltpu.VMEM((144, length), BF16),
+            pltpu.VMEM((128, length), BF16),
+            pltpu.VMEM((length, 144), BF16),
+            pltpu.VMEM((length, 128), BF16),
+            pltpu.VMEM((64, length), BF16),
+            pltpu.VMEM((length, 128), BF16),
+            pltpu.VMEM((64, length), F32),
+            heads(64, rows),
+            heads(rows, 128),
+            heads(rows, 128),
+            pltpu.VMEM((rows, width), BF16),
+            pltpu.VMEM((rows, width), BF16),
+            heads(16, mlp_part),
+            heads(16, mlp_part),
+            total(mlp_part),
+            heads(16, att_part),
+            heads(16, att_part),
+            total(att_part),
+            sems(14),
+            sems(2, 11),
+            sems(2, 7),
+            sems(2, peers),
+            sems(2, peers),
+            sems(2, peers),
+            sems(2, peers),
+            sems(2, peers),
+            sems(2, peers),
+            sems(4, peers),
+            sems(4, peers),
+        ],
+        compiler_params=pltpu.CompilerParams(
+            collective_id=0, has_side_effects=True, vmem_limit_bytes=VMEM_LIMIT
+        ),
+        name="run_layer",
+    )(index, tokens, cotangent, *weights, *tables, biases, value_bias, hidden_bias, gains)
+
+
+def heads_body(
+    tokens,
+    cotangent,
+    sequence_adapter_index,
+    query_key_value_weight,
+    output_weight,
+    first_feed_weight,
+    second_feed_weight,
+    biases,
+    value_bias_vector,
+    first_feed_bias,
+    norm_gain_pair,
+    adapter_down_factors,
+    output_down_factor,
+    adapter_up_factors,
+    hidden_up_factor,
+    hidden_down_factor,
+):
+    width = tokens.shape[2]
+    hidden = first_feed_bias.shape[0]
+    adapter_number = adapter_down_factors.shape[0]
+    outcome, grad_tokens, index_all, term_hd, term_uh, term_down, term_up, term_do, *_ = run_layer(
+        sequence_adapter_index,
+        tokens[0],
+        cotangent[0],
+        (query_key_value_weight, output_weight, first_feed_weight, second_feed_weight),
+        (
+            adapter_down_factors.reshape(-1, width),
+            adapter_up_factors.reshape(-1, width),
+            output_down_factor.reshape(-1, width),
+            hidden_up_factor.reshape(-1, hidden),
+            hidden_down_factor.reshape(-1, hidden),
+        ),
+        biases,
+        value_bias_vector[None],
+        first_feed_bias[None],
+        norm_gain_pair,
+    )
+    picker = index_all[:, 0, :1] == jnp.arange(adapter_number, dtype=F32)[None, :]
+    tables = []
+    for every in (term_down, term_do, term_up, term_uh, term_hd):
+        table = 0.0
+        for seq in range(2):
+            mask = picker[seq].reshape((adapter_number,) + (1,) * (every.ndim - 1))
+            table = table + jnp.where(mask, every[seq][None].astype(F32), 0.0)
+        tables.append(table)
+    return (outcome[None], grad_tokens[None], *tables)
+
+
 def solution(mesh):
+    one_head_each = mesh.shape["ctx"] == H and mesh.shape["fsdp"] == 2
     return jax.shard_map(
-        body,
+        heads_body if one_head_each else gather_body,
         mesh=mesh,
         in_specs=(
             P("fsdp", "ctx", None),

time: 1090 us -> 190 us (0.17)
  waiting for transfers between devices: 697 us -> 0 us
  matrix products: 247 us -> 0 us
  Pallas kernels: 0 us -> 177 us
  local copies, waits for them, and re-layouts: 81.7 us -> 2.59 us
  other arithmetic: 30.3 us -> 8.56 us
  between operations: 15.8 us -> 1.34 us
  loops' own time: 11.6 us -> 0 us
    reduce_scatter x2 -> x0, waiting for transfers between devices: 330 us -> none  [the longest x1 183 us: body(): lax.psum_scatter(grad_key_all.reshape(seq_count, length, model_width).ast...]
    dot_general x93 -> x0, matrix products: 247 us -> none  [the longest x76 204 us: plain_sum(): return jnp.einsum(form, left, right, preferred_element_type=jnp.float32)]
    psum x1 -> x0, waiting for transfers between devices: 189 us -> none  [body(): lax.psum((mlp_hup, mlp_hdown, mlp_fc1, mlp_fc2), ('ctx', 'fsdp'))]
    pallas_call x0 -> x1, Pallas kernels: none -> 177 us  [run_layer(): pl.pallas_call(functools.partial(layer_kernel, block_q, block_k), out_sha...]
    all_gather x6 -> x0, waiting for transfers between devices: 175 us -> none  [the longest x1 100 us: body(): lax.all_gather(keys_own, 'ctx', axis=1, tiled=True)]
    convert_element_type x4 -> x0, local copies, waits for them, and re-layouts: 25.4 us -> none  [the longest x1 12 us: body(): grad_key_all.reshape(seq_count, length, model_width).astype(jnp.bfloat16)]
    all_gather x2 -> x0, local copies, waits for them, and re-layouts: 23.9 us -> none  [the longest x1 12.1 us: body(): lax.all_gather(values_own, 'ctx', axis=1, tiled=True)]
    reduce_sum x13 -> x0, other arithmetic: 12.5 us -> none  [the longest x8 8.93 us: max_step(): jnp.sum(jnp.exp(scores - new_max[..., None]), -1)]
  transfers between devices with their start and end apart: 9 -> 0, of which waited for: 6 -> 0; matrix products, arithmetic and copies ran while one was open for 17% -> 0% of each run, Pallas kernels for 0% -> 0%
where the time goes in v4:
time: 190 us
  Pallas kernels  177 us (93%)
  other arithmetic  8.56 us (5%)
  local copies, waits for them, and re-layouts  2.59 us (1%)
    pallas_call x1, Pallas kernels, run_layer(): pl.pallas_call(functools.partial(layer_kernel, block_q, block_k), out_sha...  177 us
    add x4, other arithmetic, heads_body(): table = table + jnp.where(mask, every[seq][None].astype(F32), 0.0)  7.2 us

profile of v4, /device:TPU:0, one launch (start us, length us, event | category | flops | bytes accessed | tf_op | source)
XLA Modules:
  0.0 189.5 jit_solution(5797843570551622580)
XLA Ops:
  1.3 177.0 %run_layer.1 = (bf16[256,1024]{1,0:T(8,128)(2,1)}, f32[256,1024]{1,0:T(8,128)}, f32[2,8,128]{2,1,0:T(8,128)}, bf16[2,16,4096]{2,1,0:T(8,128)(2,1)}, bf16[2,16,40...) custom-call(s32[1]{0:T(128)S(6)} %copy.25.index_ref, ...), custom_call_target="tpu_custom_call" | custom-call | tf_op jit(solution)/shard_map/run_layer/pallas_call | solution.py:1105
  178.3 1.2 bitcast_convert_fusion.3
  179.5 0.8 slice_reduce_fusion
  180.3 0.1 iota_compare_fusion
  180.4 0.0 copy-start.2
  180.4 2.7 %select_add_fusion.1 = (f32[8,16,4096]{2,1,0:T(8,128)}, f32[8,16,4096]{2,1,0:T(8,128)}) fusion(f32[16,4096]{1,0:T(8,128)S(1)} %get-tuple-element.26, f32[16,4096]{1,0:T(8,128)S(1)} %get-tuple-element.25, pred[8]{0:T(512)(128)(4,1)S(1)} %get-tuple-element.36, pred[8]{0:T(512)(128)(4,1)S(1)} %get-tuple-element.35, f32[16,4096]{1,0:T(8,128)S(1)} %get-tuple-element.37, ...), kind=kLoop, calls=%fused_computation.1 | loop fusion | flops 3145728 | bytes 5242896 | tf_op jit(solution)/shard_map/add | solution.py:1219
  183.0 0.0 copy-done.2
  183.0 0.0 copy-start.4
  183.0 0.1 bitcast_convert_fusion.1
  183.1 0.0 copy-start.3
  183.1 1.9 %select_add_fusion = f32[8,5,16,1024]{3,2,1,0:T(8,128)} fusion(f32[5,16,1024]{2,1,0:T(8,128)S(1)} %get-tuple-element.24, f32[5,16,1024]{2,1,0:T(8,128)S(1)} %get-tuple-element.23, pred[8]{0:T(512)(128)(4,1)S(1)} %get-tuple-element.36, pred[8]{0:T(512)(128)(4,1)S(1)} %get-tuple-element.35), kind=kLoop, calls=%fused_computation | loop fusion | flops 1966080 | bytes 3276816 | tf_op jit(solution)/shard_map/add | solution.py:1219
  185.1 0.0 copy-done.4
  185.1 0.0 copy-start.1
  185.1 0.9 select_add_fusion.4
  186.0 0.0 copy-done.3
  186.0 0.0 copy-start
  186.1 1.7 select_add_fusion.3
  187.7 0.0 copy-done.1
  187.7 0.8 copy.26
  188.5 0.0 copy-done
  188.5 1.0 copy.27
  (3 shorter events, 0.1 us)
Async XLA Ops:
  180.4 2.7 %copy-start.2 = (bf16[2,5,16,1024]{3,2,1,0:T(8,128)(2,1)S(1)}, bf16[2,5,16,1024]{3,2,1,0:T(8,128)(2,1)}, u32[]{:S(2)}) copy-start(bf16[2,5,16,1024]{3,2,1,0:T(8,128)(2,1)} %get-tuple-element.20) | copy-start | bytes 983044
  183.0 2.0 %copy-start.4 = (bf16[2,16,1024]{2,1,0:T(8,128)(2,1)S(1)}, bf16[2,16,1024]{2,1,0:T(8,128)(2,1)}, u32[]{:S(2)}) copy-start(bf16[2,16,1024]{2,1,0:T(8,128)(2,1)} %get-tuple-element.19) | copy-start | bytes 196612
  183.1 2.9 %copy-start.3 = (bf16[2,4,16,1024]{3,2,1,0:T(8,128)(2,1)S(1)}, bf16[2,4,16,1024]{3,2,1,0:T(8,128)(2,1)}, u32[]{:S(2)}) copy-start(bf16[2,4,16,1024]{3,2,1,0:T(8,128)(2,1)} %get-tuple-element.18) | copy-start | bytes 786436
  185.1 2.7 %copy-start.1 = (bf16[256,1024]{1,0:T(8,128)(2,1)S(1)}, bf16[256,1024]{1,0:T(8,128)(2,1)}, u32[]{:S(2)}) copy-start(bf16[256,1024]{1,0:T(8,128)(2,1)} %get-tuple-element.15) | copy-start | bytes 1572868
  186.0 2.5 %copy-start = (f32[256,1024]{1,0:T(8,128)S(1)}, f32[256,1024]{1,0:T(8,128)}, u32[]{:S(2)}) copy-start(f32[256,1024]{1,0:T(8,128)} %get-tuple-element.16) | copy-start | bytes 3145732
